TPU v7x, 256 devices: a whole 4x4x8 slice. The times are simulated.
256 devices in a mesh: merge: 8 (over y, core), grp: 32 (over z, x).
Axes of the slice: x: 4, y: 4, z: 8, core: 2. Of those that a mesh axis runs over, the one named last changes fastest.
Arguments:
- child_vectors: bfloat16 [16, 2048, 2048], P('merge', 'grp'), parts along dimension 0, may hold values from -0.125 to 0.125
- child_values: float32 [32768], P('merge'), parts along dimension 0, may hold values from -2 to 2, as said below
- deflated: int32 [32768], P('merge'), parts along dimension 0, may hold values from 0 to 1, as said below
- order: int32 [32768], P('merge'), parts along dimension 0, may hold values from 0 to 4095, as said below
- coupling: float32 [8], P('merge'), parts along dimension 0, may hold values from 0.5 to 2
Outputs:
- eigenvalues: float32 [32768], P(('merge', 'grp')), parts along dimension 0
- eigenvectors: bfloat16 [32768, 4096], P('merge', 'grp'), parts along dimension 0
There are 8 independent parts, one for each index of `merge`. A program takes and returns all parts, laid end to end along the dimension named above; each array names one. Nothing has to cross between parts.
Inputs may be any that keep to these rules, and one draw needn't show every extreme that they name: `child_values`: within each child (2048 values each) the values ascend; all 4096 values are distinct and any two differ by more than 1.6 / 4096. 1 marks a deflated eigenvalue. Every index appears once: first the indices with deflated 0 in ascending order of child_values, then those with deflated 1 in ascending order of child_values.
All inputs are finite; a program needn't handle non-finite values.
Results may differ from a plain program's by a relative error of at most 0.0034.
Values may be sent and summed in bfloat16 or wider, within the bound.
No kernel may reach another device: no remote copies, remote signals or barrier semaphores. Data moves between devices by JAX's collectives and lax.ppermute only.
A program may use at most 64 MiB of HBM per device.

v0:
```python
import jax
import jax.numpy as jnp
from jax import lax
from jax.sharding import PartitionSpec as P

ITERS = 4


margin = 0.05


def secular_roots(indices, values, living, ordering, weights, coupled):
    full_order = values.shape[0]
    position = (
        jnp.zeros((full_order,), jnp.int32)
        .at[ordering]
        .set(jnp.arange(full_order, dtype=jnp.int32))
    )
    nonzero = jnp.sum(living.astype(jnp.int32))
    places = position[indices]
    successor = ordering[jnp.minimum(places + 1, full_order - 1)]
    anchor = values[indices]
    living_rows = living[indices]
    ceiling = jnp.where(
        places == nonzero - 1, anchor + coupled * jnp.sum(weights), values[successor]
    )
    spacing = ceiling - anchor
    offsets = values[None, :] - anchor[:, None]
    paired = living_rows[:, None] & living[None, :]
    shifts = 0.5 * spacing
    for sweep_index in range(ITERS):
        gapped = jnp.where(paired, offsets - shifts[:, None], 1.0)
        inverse = 1.0 / gapped
        partial_terms = weights[None, :] * inverse
        residue = 1.0 / coupled + jnp.sum(partial_terms, axis=1)
        derivative = jnp.where(living_rows, jnp.sum(partial_terms * inverse, axis=1), 1.0)
        shifts = jnp.clip(shifts - residue / derivative, margin * spacing, (1.0 - margin) * spacing)
    return jnp.where(living_rows, shifts, 0.0)


def loewner_logs(indices, shifts, values, living):
    full_order = values.shape[0]
    offsets = values[None, :] - values[indices][:, None]
    diagonal = indices[:, None] == jnp.arange(full_order, dtype=jnp.int32)[None, :]
    paired = living[indices][:, None] & living[None, :]
    numerator = jnp.where(paired, jnp.abs(offsets - shifts[:, None]), 1.0)
    denominator = jnp.where(paired & ~diagonal, jnp.abs(offsets), 1.0)
    return jnp.sum(jnp.log(numerator) - jnp.log(denominator), axis=0)


def weights_hat(log_totals, zvector, living, coupled):
    sign_values = jnp.where(zvector >= 0, 1.0, -1.0)
    return jnp.where(living, sign_values * jnp.sqrt(jnp.exp(log_totals) / coupled), 0.0)


def basis_columns(indices, shifts, values, living, hat_weights):
    full_order = values.shape[0]
    offsets = values[:, None] - values[indices][None, :]
    living_cols = living[indices]
    paired = living[:, None] & living_cols[None, :]
    vectors = hat_weights[:, None] / jnp.where(paired, offsets - shifts[None, :], 1.0)
    lengths = jnp.where(living_cols, jnp.sqrt(jnp.sum(vectors * vectors, axis=0)), 1.0)
    identity = (jnp.arange(full_order, dtype=jnp.int32)[:, None] == indices[None, :]).astype(
        values.dtype
    )
    return jnp.where(living_cols[None, :], vectors / lengths[None, :], identity)


def local(child_vectors, child_values, deflated, order, coupling):
    half_order = child_vectors.shape[2]
    full_order = 2 * half_order
    group_size = lax.axis_size("grp")
    column_share = full_order // group_size
    local_rows = child_vectors.shape[1]
    member = lax.axis_index("grp")
    living = deflated == 0
    coupled = coupling[0]
    first_edge = jnp.where(
        member == group_size - 1, child_vectors[0, local_rows - 1, :].astype(jnp.float32), 0.0
    )
    second_edge = jnp.where(member == 0, child_vectors[1, 0, :].astype(jnp.float32), 0.0)
    boundary = lax.psum(jnp.concatenate([first_edge, second_edge]), "grp")
    zvector = jnp.where(living, boundary, 0.0)
    weights = zvector * zvector
    own_columns = member * column_share + jnp.arange(column_share, dtype=jnp.int32)
    own_shifts = secular_roots(own_columns, child_values, living, order, weights, coupled)
    eigenvalues = child_values[own_columns] + own_shifts
    block_size = min(512, full_order)
    rounds = full_order // block_size
    all_shifts = own_shifts
    all_shifts = lax.all_gather(own_shifts, "grp", axis=0, tiled=True)

    def add_block(block_index, running):
        block_start = block_index * block_size
        indices = block_start + jnp.arange(block_size, dtype=jnp.int32)
        shifts = lax.dynamic_slice_in_dim(all_shifts, block_start, block_size)
        return running + loewner_logs(indices, shifts, child_values, living)

    log_totals = lax.fori_loop(0, rounds, add_block, jnp.zeros((full_order,), jnp.float32))
    hat_weights = weights_hat(log_totals, zvector, living, coupled)

    def fill_block(block_index, buffer):
        block_start = block_index * block_size
        indices = block_start + jnp.arange(block_size, dtype=jnp.int32)
        shifts = lax.dynamic_slice_in_dim(all_shifts, block_start, block_size)
        merged_basis = basis_columns(indices, shifts, child_values, living, hat_weights).astype(
            jnp.bfloat16
        )
        upper_part = jnp.dot(
            child_vectors[0], merged_basis[:half_order], preferred_element_type=jnp.float32
        )
        lower_part = jnp.dot(
            child_vectors[1], merged_basis[half_order:], preferred_element_type=jnp.float32
        )
        produced = jnp.stack([upper_part, lower_part]).astype(jnp.bfloat16)
        return lax.dynamic_update_slice_in_dim(buffer, produced, block_start, 2)

    out_rows = lax.fori_loop(
        0, rounds, fill_block, jnp.zeros((2, local_rows, full_order), jnp.bfloat16)
    )
    returned = lax.all_to_all(out_rows, "grp", split_axis=2, concat_axis=1, tiled=True)
    eigenvectors = returned.reshape(full_order, column_share)
    return (eigenvalues, eigenvectors)


def solution(mesh):
    in_specs = (P("merge", "grp", None), P("merge"), P("merge"), P("merge"), P("merge"))
    out_specs = (P(("merge", "grp")), P("merge", "grp"))
    return jax.shard_map(local, mesh=mesh, in_specs=in_specs, out_specs=out_specs, check_vma=False)
```

profile of v0, /device:TPU:26, one launch (start us, length us, event | category | flops | bytes accessed | tf_op | source)
XLA Modules:
  0.0 490.3 jit_solution(4540219757311322092)
XLA Ops:
  6.4 140.6 %psum.7 = f32[4096]{0:T(1024)S(1)} all-reduce(f32[4096]{0:T(1024)S(1)} %pad_maximum_fusion), channel_id=1, replica_groups=mesh['merge'=8,'grp'=32] {'grp'}, use_global_device_ids=true, to_apply=%region_2.3 | all-reduce | flops 4096 | bytes 32768 | tf_op jit(solution)/shard_map/psum | solution.py:82
  147.8 15.5 %scatter_custom_fusion = s32[4096]{0:T(1024)S(1)} fusion(s32[4096]{0:T(1024)S(1)} %compare_select_fusion.2, s32[4096]{0:T(1024)S(1)} %iota.52, s32[]{:T(128)} %constant.109.clone.1), kind=kCustom, calls=%fused_computation.78 | custom fusion | bytes 16388 | tf_op jit(solution)/shard_map/scatter | solution.py:17
  172.9 40.3 %all-gather = f32[32,1,128]{2,1,0:T(1,128)S(1)} all-gather(f32[1,1,128]{2,1,0:T(1,128)S(1)} %bitcast.61), channel_id=1, replica_groups=mesh['merge'=8,'grp'=32] {'grp'}, dimensions={0}, use_global_device_ids=true | all-gather | bytes 16896 | tf_op jit(solution)/shard_map/all_gather | solution.py:91
  213.2 106.8 %while.28 = (s32[]{:T(128)}, f32[4096]{0:T(1024)S(1)}, pred[4096]{0:T(1024)(128)(4,1)S(1)}, f32[4096]{0:T(1024)S(1)}, f32[4096]{0:T(1024)S(1)}, /*index=5*/s32[]{:T(128)}, s32[]{:T(128)}, s32[]{:T(128)}, s32[]{:T(128)}) while((s32[]{:T(128)}, f32[4096]{0:T(1024)S(1)}, pred[4096]{0:T(1024)(128)(4,1)S(1)}, f32[4096]{0:T(1024)S(1)}, ...), condition=%wide.region_14.15_spmd.clone, body=%wide.region_12.14_spmd.clone.sunk | while | flops 25173508 | bytes 116393 | solution.py:99
  213.3 3.5 gather_fusion.3
  219.9 6.5 %fusion.57 = f32[4096]{0:T(1024)S(1)} fusion(s32[512]{0:T(512)S(1)} %iota_add_fusion.5, f32[512]{0:T(512)S(1)} %dynamic_slice.18, f32[512]{0:T(512)S(1)} %gather_fusion.2, f32[4096]{0:T(1024)S(1)} %get-tuple-element.377, pred[4096]{0:T(1024)(128)(4,1)S(1)} %get-tuple-element.376, pred[512]{0:T(512)(128)(4,1)S(1)} %gather_fusion.3), kind=kLoop, calls=%fused_computation.37.clone.1 | loop fusion | flops 25161728 | bytes 43520 | tf_op jit(solution)/shard_map/while/body/eval_jaxpr/reduce_sum | solution.py:48
  226.6 3.5 gather_fusion.3
  233.3 6.5 %fusion.57 = f32[4096]{0:T(1024)S(1)} fusion(s32[512]{0:T(512)S(1)} %iota_add_fusion.5, f32[512]{0:T(512)S(1)} %dynamic_slice.18, f32[512]{0:T(512)S(1)} %gather_fusion.2, f32[4096]{0:T(1024)S(1)} %get-tuple-element.377, pred[4096]{0:T(1024)(128)(4,1)S(1)} %get-tuple-element.376, pred[512]{0:T(512)(128)(4,1)S(1)} %gather_fusion.3), kind=kLoop, calls=%fused_computation.37.clone.1 | loop fusion | flops 25161728 | bytes 43520 | tf_op jit(solution)/shard_map/while/body/eval_jaxpr/reduce_sum | solution.py:48
  246.6 6.5 %fusion.57 = f32[4096]{0:T(1024)S(1)} fusion(s32[512]{0:T(512)S(1)} %iota_add_fusion.5, f32[512]{0:T(512)S(1)} %dynamic_slice.18, f32[512]{0:T(512)S(1)} %gather_fusion.2, f32[4096]{0:T(1024)S(1)} %get-tuple-element.377, pred[4096]{0:T(1024)(128)(4,1)S(1)} %get-tuple-element.376, pred[512]{0:T(512)(128)(4,1)S(1)} %gather_fusion.3), kind=kLoop, calls=%fused_computation.37.clone.1 | loop fusion | flops 25161728 | bytes 43520 | tf_op jit(solution)/shard_map/while/body/eval_jaxpr/reduce_sum | solution.py:48
  253.3 3.5 gather_fusion.3
  260.0 6.5 %fusion.57 = f32[4096]{0:T(1024)S(1)} fusion(s32[512]{0:T(512)S(1)} %iota_add_fusion.5, f32[512]{0:T(512)S(1)} %dynamic_slice.18, f32[512]{0:T(512)S(1)} %gather_fusion.2, f32[4096]{0:T(1024)S(1)} %get-tuple-element.377, pred[4096]{0:T(1024)(128)(4,1)S(1)} %get-tuple-element.376, pred[512]{0:T(512)(128)(4,1)S(1)} %gather_fusion.3), kind=kLoop, calls=%fused_computation.37.clone.1 | loop fusion | flops 25161728 | bytes 43520 | tf_op jit(solution)/shard_map/while/body/eval_jaxpr/reduce_sum | solution.py:48
  266.7 3.5 gather_fusion.3
  273.4 6.5 %fusion.57 = f32[4096]{0:T(1024)S(1)} fusion(s32[512]{0:T(512)S(1)} %iota_add_fusion.5, f32[512]{0:T(512)S(1)} %dynamic_slice.18, f32[512]{0:T(512)S(1)} %gather_fusion.2, f32[4096]{0:T(1024)S(1)} %get-tuple-element.377, pred[4096]{0:T(1024)(128)(4,1)S(1)} %get-tuple-element.376, pred[512]{0:T(512)(128)(4,1)S(1)} %gather_fusion.3), kind=kLoop, calls=%fused_computation.37.clone.1 | loop fusion | flops 25161728 | bytes 43520 | tf_op jit(solution)/shard_map/while/body/eval_jaxpr/reduce_sum | solution.py:48
  280.0 3.5 gather_fusion.3
  286.7 6.5 %fusion.57 = f32[4096]{0:T(1024)S(1)} fusion(s32[512]{0:T(512)S(1)} %iota_add_fusion.5, f32[512]{0:T(512)S(1)} %dynamic_slice.18, f32[512]{0:T(512)S(1)} %gather_fusion.2, f32[4096]{0:T(1024)S(1)} %get-tuple-element.377, pred[4096]{0:T(1024)(128)(4,1)S(1)} %get-tuple-element.376, pred[512]{0:T(512)(128)(4,1)S(1)} %gather_fusion.3), kind=kLoop, calls=%fused_computation.37.clone.1 | loop fusion | flops 25161728 | bytes 43520 | tf_op jit(solution)/shard_map/while/body/eval_jaxpr/reduce_sum | solution.py:48
  293.4 3.5 gather_fusion.3
  300.1 6.5 %fusion.57 = f32[4096]{0:T(1024)S(1)} fusion(s32[512]{0:T(512)S(1)} %iota_add_fusion.5, f32[512]{0:T(512)S(1)} %dynamic_slice.18, f32[512]{0:T(512)S(1)} %gather_fusion.2, f32[4096]{0:T(1024)S(1)} %get-tuple-element.377, pred[4096]{0:T(1024)(128)(4,1)S(1)} %get-tuple-element.376, pred[512]{0:T(512)(128)(4,1)S(1)} %gather_fusion.3), kind=kLoop, calls=%fused_computation.37.clone.1 | loop fusion | flops 25161728 | bytes 43520 | tf_op jit(solution)/shard_map/while/body/eval_jaxpr/reduce_sum | solution.py:48
  306.8 3.5 gather_fusion.3
  313.4 6.5 %fusion.57 = f32[4096]{0:T(1024)S(1)} fusion(s32[512]{0:T(512)S(1)} %iota_add_fusion.5, f32[512]{0:T(512)S(1)} %dynamic_slice.18, f32[512]{0:T(512)S(1)} %gather_fusion.2, f32[4096]{0:T(1024)S(1)} %get-tuple-element.377, pred[4096]{0:T(1024)(128)(4,1)S(1)} %get-tuple-element.376, pred[512]{0:T(512)(128)(4,1)S(1)} %gather_fusion.3), kind=kLoop, calls=%fused_computation.37.clone.1 | loop fusion | flops 25161728 | bytes 43520 | tf_op jit(solution)/shard_map/while/body/eval_jaxpr/reduce_sum | solution.py:48
  320.1 135.2 %while.27 = (s32[]{:T(128)}, bf16[2,64,4096]{2,1,0:T(8,128)(2,1)S(1)}, pred[4096]{0:T(1024)(128)(4,1)S(1)}, f32[4096]{0:T(1024)S(1)}, f32[4096]{0:T(1024)S(1)}, ...) while((s32[]{:T(128)}, ...), condition=%wide.region_17.18_spmd, body=%wide.region_15.17_spmd.sunk | while | flops 304418304 | bytes 9423531 | solution.py:118
  320.3 3.5 gather_fusion
  330.3 5.7 %select_convert_fusion.2 = bf16[4096,512]{1,0:T(8,128)(2,1)S(1)} fusion(s32[512]{0:T(512)S(1)} %iota_add_fusion.4, f32[512]{0:T(512)S(1)} %sqrt_select_fusion.2, f32[512]{0:T(512)S(1)} %dynamic_slice.17, f32[512]{0:T(512)S(1)} %gather_fusion.1, f32[4096]{0:T(1024)S(1)} %get-tuple-element.409, f32[4096]{0:T(1024)S(1)} %get-tuple-element.408, ...), kind=kLoop, calls=%fused_computation.10.clone.1 | loop fusion | flops 20971520 | bytes 4239872 | tf_op jit(solution)/shard_map/while/body/eval_jaxpr/convert_element_type | solution.py:106
  337.2 3.5 gather_fusion
  347.3 5.7 %select_convert_fusion.2 = bf16[4096,512]{1,0:T(8,128)(2,1)S(1)} fusion(s32[512]{0:T(512)S(1)} %iota_add_fusion.4, f32[512]{0:T(512)S(1)} %sqrt_select_fusion.2, f32[512]{0:T(512)S(1)} %dynamic_slice.17, f32[512]{0:T(512)S(1)} %gather_fusion.1, f32[4096]{0:T(1024)S(1)} %get-tuple-element.409, f32[4096]{0:T(1024)S(1)} %get-tuple-element.408, ...), kind=kLoop, calls=%fused_computation.10.clone.1 | loop fusion | flops 20971520 | bytes 4239872 | tf_op jit(solution)/shard_map/while/body/eval_jaxpr/convert_element_type | solution.py:106
  364.2 5.7 %select_convert_fusion.2 = bf16[4096,512]{1,0:T(8,128)(2,1)S(1)} fusion(s32[512]{0:T(512)S(1)} %iota_add_fusion.4, f32[512]{0:T(512)S(1)} %sqrt_select_fusion.2, f32[512]{0:T(512)S(1)} %dynamic_slice.17, f32[512]{0:T(512)S(1)} %gather_fusion.1, f32[4096]{0:T(1024)S(1)} %get-tuple-element.409, f32[4096]{0:T(1024)S(1)} %get-tuple-element.408, ...), kind=kLoop, calls=%fused_computation.10.clone.1 | loop fusion | flops 20971520 | bytes 4239872 | tf_op jit(solution)/shard_map/while/body/eval_jaxpr/convert_element_type | solution.py:106
  381.1 5.7 %select_convert_fusion.2 = bf16[4096,512]{1,0:T(8,128)(2,1)S(1)} fusion(s32[512]{0:T(512)S(1)} %iota_add_fusion.4, f32[512]{0:T(512)S(1)} %sqrt_select_fusion.2, f32[512]{0:T(512)S(1)} %dynamic_slice.17, f32[512]{0:T(512)S(1)} %gather_fusion.1, f32[4096]{0:T(1024)S(1)} %get-tuple-element.409, f32[4096]{0:T(1024)S(1)} %get-tuple-element.408, ...), kind=kLoop, calls=%fused_computation.10.clone.1 | loop fusion | flops 20971520 | bytes 4239872 | tf_op jit(solution)/shard_map/while/body/eval_jaxpr/convert_element_type | solution.py:106
  398.0 5.7 %select_convert_fusion.2 = bf16[4096,512]{1,0:T(8,128)(2,1)S(1)} fusion(s32[512]{0:T(512)S(1)} %iota_add_fusion.4, f32[512]{0:T(512)S(1)} %sqrt_select_fusion.2, f32[512]{0:T(512)S(1)} %dynamic_slice.17, f32[512]{0:T(512)S(1)} %gather_fusion.1, f32[4096]{0:T(1024)S(1)} %get-tuple-element.409, f32[4096]{0:T(1024)S(1)} %get-tuple-element.408, ...), kind=kLoop, calls=%fused_computation.10.clone.1 | loop fusion | flops 20971520 | bytes 4239872 | tf_op jit(solution)/shard_map/while/body/eval_jaxpr/convert_element_type | solution.py:106
  414.9 5.7 %select_convert_fusion.2 = bf16[4096,512]{1,0:T(8,128)(2,1)S(1)} fusion(s32[512]{0:T(512)S(1)} %iota_add_fusion.4, f32[512]{0:T(512)S(1)} %sqrt_select_fusion.2, f32[512]{0:T(512)S(1)} %dynamic_slice.17, f32[512]{0:T(512)S(1)} %gather_fusion.1, f32[4096]{0:T(1024)S(1)} %get-tuple-element.409, f32[4096]{0:T(1024)S(1)} %get-tuple-element.408, ...), kind=kLoop, calls=%fused_computation.10.clone.1 | loop fusion | flops 20971520 | bytes 4239872 | tf_op jit(solution)/shard_map/while/body/eval_jaxpr/convert_element_type | solution.py:106
  431.8 5.7 %select_convert_fusion.2 = bf16[4096,512]{1,0:T(8,128)(2,1)S(1)} fusion(s32[512]{0:T(512)S(1)} %iota_add_fusion.4, f32[512]{0:T(512)S(1)} %sqrt_select_fusion.2, f32[512]{0:T(512)S(1)} %dynamic_slice.17, f32[512]{0:T(512)S(1)} %gather_fusion.1, f32[4096]{0:T(1024)S(1)} %get-tuple-element.409, f32[4096]{0:T(1024)S(1)} %get-tuple-element.408, ...), kind=kLoop, calls=%fused_computation.10.clone.1 | loop fusion | flops 20971520 | bytes 4239872 | tf_op jit(solution)/shard_map/while/body/eval_jaxpr/convert_element_type | solution.py:106
  448.7 5.7 %select_convert_fusion.2 = bf16[4096,512]{1,0:T(8,128)(2,1)S(1)} fusion(s32[512]{0:T(512)S(1)} %iota_add_fusion.4, f32[512]{0:T(512)S(1)} %sqrt_select_fusion.2, f32[512]{0:T(512)S(1)} %dynamic_slice.17, f32[512]{0:T(512)S(1)} %gather_fusion.1, f32[4096]{0:T(1024)S(1)} %get-tuple-element.409, f32[4096]{0:T(1024)S(1)} %get-tuple-element.408, ...), kind=kLoop, calls=%fused_computation.10.clone.1 | loop fusion | flops 20971520 | bytes 4239872 | tf_op jit(solution)/shard_map/while/body/eval_jaxpr/convert_element_type | solution.py:106
  459.7 25.4 %all_to_all.15 = bf16[32,2,8192]{2,1,0:T(2,128)(2,1)S(1)} all-to-all(bf16[32,2,8192]{2,1,0:T(2,128)(2,1)S(1)} %reshape.302), channel_id=1, replica_groups=mesh['merge'=8,'grp'=32] {'grp'}, dimensions={0} | all-to-all | bytes 2097152 | tf_op jit(solution)/shard_map/all_to_all | solution.py:121
  486.5 3.9 copy.12
  (173 shorter events, 131.2 us)
Async XLA Ops:
  0.6 165.1 %copy-start = (f32[4096]{0:T(1024)S(1)}, f32[4096]{0:T(1024)}, u32[]{:S(2)}) copy-start(f32[4096]{0:T(1024)} %param.10) | copy-start | bytes 49156
  0.6 163.9 %copy-start.1 = (s32[4096]{0:T(1024)S(1)}, s32[4096]{0:T(1024)}, u32[]{:S(2)}) copy-start(s32[4096]{0:T(1024)} %param.12) | copy-start | bytes 49156
  213.2 107.0 %copy-start.2 = (bf16[2,64,2048]{2,1,0:T(8,128)(2,1)S(1)}, bf16[2,64,2048]{2,1,0:T(8,128)(2,1)}, u32[]{:S(2)}) copy-start(bf16[2,64,2048]{2,1,0:T(8,128)(2,1)} %param.9) | copy-start | bytes 1572868
where the time goes:
time: 491 us; the launch traced here: 490 us
  blocking collectives  206 us (42%)
  local copies, waits for them, and re-layouts  139 us (28%)
  other arithmetic  133 us (27%)
  matrix products  7.62 us (2%)
    psum x1, blocking collectives, local(): boundary = lax.psum(jnp.concatenate([first_edge, second_edge]), 'grp')  141 us
    reduce_sum x8, other arithmetic, loewner_logs(): return jnp.sum(jnp.log(numerator) - jnp.log(denominator), axis=0)  52.3 us
    convert_element_type x8, other arithmetic, fill_block(): basis_columns(indices, shifts, child_values, living, hat_weights)  45.5 us
    all_gather x1, blocking collectives, local(): all_shifts = lax.all_gather(own_shifts, 'grp', axis=0, tiled=True)  40.3 us
    gather x8, local copies, waits for them, and re-layouts, loewner_logs(): paired = living[indices][:, None] & living[None, :]  28.1 us
    gather x8, local copies, waits for them, and re-layouts, basis_columns(): living_cols = living[indices]  28.1 us
    reduce_sum x8, other arithmetic, basis_columns(): jnp.sum(vectors * vectors, axis=0)  27.2 us
    all_to_all x1, blocking collectives, local(): lax.all_to_all(out_rows, 'grp', split_axis=2, concat_axis=1, tiled=True)  25.4 us

commit v1 on v0

v1 whole, which is shorter than its diff:
```python
import jax
import jax.numpy as jnp
from jax import lax
from jax.experimental import pallas as pl
from jax.experimental.pallas import tpu as pltpu
from jax.sharding import Mesh, PartitionSpec as P

ITERS = 4
MARGIN = 0.05
FAR = 1.0e6
LANES = 128


def column_of(row):
    n = row.shape[1]
    eye = lax.broadcasted_iota(jnp.int32, (n, n), 0) == lax.broadcasted_iota(jnp.int32, (n, n), 1)
    return jnp.sum(jnp.where(eye, row, 0.0), axis=1, keepdims=True)


def row_of(column):
    n = column.shape[0]
    eye = lax.broadcasted_iota(jnp.int32, (n, n), 0) == lax.broadcasted_iota(jnp.int32, (n, n), 1)
    return jnp.sum(jnp.where(eye, column, 0.0), axis=0, keepdims=True)


def roots_kernel(place, rho_ref, edges, values, flags, out, eig, zrow_out, far, weight, dcol, prod):
    member = place[0]
    rho = rho_ref[0]
    full = values.shape[1]
    half_rows = full // 2 // LANES
    last = edges.shape[0] - 1
    lower = edges[last].astype(jnp.float32)
    upper = edges[0].astype(jnp.float32)
    for r in range(half_rows):
        weight[:, r * LANES : (r + 1) * LANES] = lower[r : r + 1, :]
        s = half_rows + r
        weight[:, s * LANES : (s + 1) * LANES] = upper[r : r + 1, :]
    live = flags[...] == 0
    z = jnp.where(live, weight[...], 0.0)
    zrow_out[...] = z
    w = z * z
    weight[...] = w
    total = jnp.sum(w)
    far[...] = jnp.where(live, values[...], FAR)
    own = pl.ds(pl.multiple_of(member * LANES, LANES), LANES)
    own_values = values[:, own]
    own_live = flags[:, own] == 0
    dcol[...] = jnp.broadcast_to(column_of(own_values), (LANES, LANES))
    prod[...] = jnp.ones_like(prod)
    rows = 32
    inv_rho = 1.0 / rho

    def group(g, _):
        di = dcol[pl.ds(pl.multiple_of(g * rows, rows), rows), :][:, :1]
        e = far[...] - di
        gap = jnp.min(jnp.where(e > 0, e, 2.0 * FAR), axis=1, keepdims=True)
        gap = jnp.where(gap > 0.5 * FAR, (di + rho * total) - di, gap)
        delta = 0.5 * gap
        for _ in range(ITERS):
            e = far[...] - di
            inverse = pltpu.reciprocal(e - delta, approx=True)
            term = weight[...] * inverse
            f = inv_rho + jnp.sum(term, axis=1, keepdims=True)
            h = jnp.sum(term * inverse, axis=1, keepdims=True)
            delta = jnp.clip(delta - f / h, MARGIN * gap, (1.0 - MARGIN) * gap)
        dcol[pl.ds(pl.multiple_of(g * rows, rows), rows), :] = jnp.broadcast_to(delta, (rows, LANES))
        return 0

    lax.fori_loop(0, LANES // rows, group, 0)
    own_delta = jnp.where(own_live, row_of(dcol[...][:, :1]), 0.0)
    eig[...] = own_values + own_delta
    dcol[...] = jnp.broadcast_to(column_of(own_delta), (LANES, LANES))
    vcol = column_of(own_values)
    for g in range(0, LANES, rows):
        num = None
        for k in range(0, rows, 8):
            di = vcol[g + k : g + k + 8, :]
            de = dcol[g + k : g + k + 8, :][:, :1]
            e = far[...] - di
            a = e - de
            b = jnp.where(e == 0, 1.0, e)
            num = a if num is None else num * a
            den = b if k == 0 else den * b
        prod[...] = prod[...] * (num * pltpu.reciprocal(den, approx=True))
    p = prod[...]
    p = p[:4] * p[4:]
    p = p[:2] * p[2:]
    p = p[:1] * p[1:]
    for r in range(full // LANES):
        out[0, r : r + 1, :] = p[:, r * LANES : (r + 1) * LANES]
    out[0, full // LANES : full // LANES + 1, :] = own_delta
    block = out[0]
    for s in range(1, out.shape[0]):
        out[s] = block


def vectors_kernel(
    place, rho_ref, parts, values, flags, zrow, own, left, right, far0, far1, out, far, zhat, basis, held, pdi, pde
):
    step = pl.program_id(0)
    x = place[1]
    nx = 4
    share = own.shape[1]
    rho = rho_ref[0]
    full = values.shape[1]
    half = full // 2
    blocks = full // LANES
    per = out.shape[0]

    @pl.when(step == 0)
    def _():
        p = parts[0, :blocks]
        for s in range(1, parts.shape[0]):
            p = p * parts[s, :blocks]
        p = jnp.sqrt(jnp.abs(p) / rho)
        for r in range(blocks):
            zhat[:, r * LANES : (r + 1) * LANES] = p[r : r + 1, :]
        live = flags[...] == 0
        zhat[...] = jnp.where(live, jnp.where(zrow[...] >= 0, zhat[...], -zhat[...]), 0.0)
        far[...] = jnp.where(live, values[...], FAR)

    for k in range(per):
        owner = (step * per + k) * nx + x
        cols = pl.ds(pl.multiple_of(owner * LANES, LANES), LANES)
        pdi[k * LANES : (k + 1) * LANES, :] = jnp.broadcast_to(column_of(values[:, cols]), (LANES, LANES))
        pde[k * LANES : (k + 1) * LANES, :] = jnp.broadcast_to(
            column_of(parts[owner, blocks : blocks + 1, :]), (LANES, LANES)
        )
    rows = 32

    def group(g, _):
        at = pl.ds(pl.multiple_of(g * rows, rows), rows)
        di = pdi[at, :]
        de = pde[at, :]
        acc = jnp.zeros((rows, LANES), jnp.float32)
        for b in range(blocks):
            sl = slice(b * LANES, (b + 1) * LANES)
            v = zhat[:, sl] * pltpu.reciprocal((far[:, sl] - di) - de, approx=True)
            acc = acc + v * v
            held[:, sl] = v
        scale = lax.rsqrt(jnp.sum(acc, axis=1, keepdims=True))
        scale = jnp.broadcast_to(scale, (rows, LANES))
        for b in range(blocks):
            sl = slice(b * LANES, (b + 1) * LANES)
            basis[at, sl] = (held[:, sl] * scale).astype(jnp.bfloat16)
        return 0

    lax.fori_loop(0, per * LANES // rows, group, 0)
    for c in range(2):
        slots = (own.at[c], left.at[c], right.at[c], (far0, far1)[c])
        lhs = jnp.concatenate([slot[...] for slot in slots], axis=0)
        rhs = basis[:, c * half : (c + 1) * half]
        acc = lax.dot_general(lhs, rhs, (((1,), (1,)), ((), ())), preferred_element_type=jnp.float32)
        for k in range(per):
            owner = (step * per + k) * nx + x
            dead = flags[:, pl.ds(pl.multiple_of(owner * LANES, LANES), LANES)] != 0
            mine = owner < blocks // 2 if c == 0 else owner >= blocks // 2
            inner = owner if c == 0 else owner - blocks // 2
            inner = jnp.where(mine, inner, 0)
            for s, slot in enumerate(slots):
                plain = slot[:, pl.ds(pl.multiple_of(inner * LANES, LANES), LANES)].astype(jnp.float32)
                plain = jnp.where(mine, plain, 0.0)
                got = acc[s * share : (s + 1) * share, k * LANES : (k + 1) * LANES]
                source = lax.rem(x + (0, nx - 1, 1, 2)[s], nx)
                out[k, c, pl.ds(pl.multiple_of(source * share, share), share), :] = jnp.where(dead, plain, got).astype(
                    jnp.bfloat16
                )


def local(child_vectors, child_values, deflated, order, coupling):
    del order
    half = child_vectors.shape[2]
    full = 2 * half
    rows = child_vectors.shape[1]
    nz, nx = lax.axis_size("z"), lax.axis_size("x")
    group = nz * nx
    z, x = lax.axis_index("z"), lax.axis_index("x")
    member = z * nx + x
    blocks = full // LANES
    whole = lambda: pl.BlockSpec(memory_space=pltpu.VMEM)
    scalar = lambda: pl.BlockSpec(memory_space=pltpu.SMEM)

    ahead = [(i, (i + 1) % nx) for i in range(nx)]
    back = [(i, (i - 1) % nx) for i in range(nx)]
    left = lax.ppermute(child_vectors, "x", ahead)
    right = lax.ppermute(child_vectors, "x", back)

    place = jnp.stack([member, x]).astype(jnp.int32)
    edge = jnp.where(member == group - 1, child_vectors[0, rows - 1], child_vectors[1, 0])
    edge = jnp.broadcast_to(edge.reshape(1, half // LANES, LANES), (group, half // LANES, LANES))
    edges = lax.all_to_all(edge, ("z", "x"), 0, 0, tiled=True)
    child_values, left, right = lax.optimization_barrier((child_values, left, right))
    opposite = (lax.ppermute(left[0], "x", ahead), lax.ppermute(right[1], "x", back))
    values = child_values.reshape(1, full)
    flags = deflated.reshape(1, full)
    parts, eig, zrow = pl.pallas_call(
        roots_kernel,
        out_shape=(
            jax.ShapeDtypeStruct((group, blocks + 8, LANES), jnp.float32),
            jax.ShapeDtypeStruct((1, LANES), jnp.float32),
            jax.ShapeDtypeStruct((1, full), jnp.float32),
        ),
        in_specs=[scalar(), scalar(), whole(), whole(), whole()],
        out_specs=(whole(), whole(), whole()),
        scratch_shapes=[
            pltpu.VMEM((1, full), jnp.float32),
            pltpu.VMEM((1, full), jnp.float32),
            pltpu.VMEM((LANES, LANES), jnp.float32),
            pltpu.VMEM((8, full), jnp.float32),
        ],
        compiler_params=pltpu.CompilerParams(vmem_limit_bytes=32 * 1024 * 1024),
        name="roots",
    )(place, coupling, edges, values, flags)
    parts = lax.all_to_all(parts, ("z", "x"), 0, 0, tiled=True)
    per = 2
    produced = pl.pallas_call(
        vectors_kernel,
        grid=(nz // per,),
        out_shape=jax.ShapeDtypeStruct((nz, 2, nx * rows, LANES), jnp.bfloat16),
        in_specs=[scalar(), scalar()] + [whole()] * 9,
        out_specs=pl.BlockSpec((per, 2, nx * rows, LANES), lambda i: (i, 0, 0, 0)),
        scratch_shapes=[
            pltpu.VMEM((1, full), jnp.float32),
            pltpu.VMEM((1, full), jnp.float32),
            pltpu.VMEM((per * LANES, full), jnp.bfloat16),
            pltpu.VMEM((32, full), jnp.float32),
            pltpu.VMEM((per * LANES, LANES), jnp.float32),
            pltpu.VMEM((per * LANES, LANES), jnp.float32),
        ],
        compiler_params=pltpu.CompilerParams(vmem_limit_bytes=40 * 1024 * 1024),
        name="vectors",
    )(place, coupling, parts, values, flags, zrow, child_vectors, left, right, *opposite)
    returned = lax.all_to_all(produced, "z", 0, 0, tiled=True)
    eigenvectors = returned.transpose(1, 0, 2, 3).reshape(full, LANES)
    return eig.reshape(LANES), eigenvectors


def solution(mesh):
    inner = Mesh(mesh.devices.reshape(mesh.devices.shape[0], -1, 4), ("merge", "z", "x"))
    grp = ("z", "x")
    in_specs = (P("merge", grp, None), P("merge"), P("merge"), P("merge"), P("merge"))
    out_specs = (P(("merge",) + grp), P("merge", grp))
    return jax.shard_map(local, mesh=inner, in_specs=in_specs, out_specs=out_specs, check_vma=False)
```

time: 491 us -> 96.9 us (0.20)
  blocking collectives: 206 us -> 28.2 us
  local copies, waits for them, and re-layouts: 139 us -> 1.77 us
  other arithmetic: 133 us -> 0.91 us
  waiting for transfers between devices: 0 us -> 23.9 us
  starting transfers between devices: 0 us -> 21.4 us
  Pallas kernels: 0 us -> 18.1 us
  matrix products: 7.62 us -> 0 us
    psum x1 -> x0, blocking collectives: 141 us -> none  [local(): boundary = lax.psum(jnp.concatenate([first_edge, second_edge]), 'grp')]
    gather x37 -> x0, local copies, waits for them, and re-layouts: 113 us -> none  [the longest x8 28.1 us: loewner_logs(): paired = living[indices][:, None] & living[None, :]]
    reduce_sum x22 -> x0, other arithmetic: 84.9 us -> none  [the longest x8 52.3 us: loewner_logs(): return jnp.sum(jnp.log(numerator) - jnp.log(denominator), axis=0)]
    convert_element_type x8 -> x0, other arithmetic: 45.5 us -> none  [fill_block(): basis_columns(indices, shifts, child_values, living, hat_weights)]
    all_gather x1 -> x0, blocking collectives: 40.3 us -> none  [local(): all_shifts = lax.all_gather(own_shifts, 'grp', axis=0, tiled=True)]
    pallas_call x0 -> x2, Pallas kernels: none -> 18.1 us  [the longest x1 11 us: local(): pl.pallas_call(vectors_kernel, grid=(nz // per,), out_shape=jax.ShapeDtyp...]
    all_to_all x0 -> x2, starting transfers between devices: none -> 17.2 us  [the longest x1 11.7 us: local(): edges = lax.all_to_all(edge, ('z', 'x'), 0, 0, tiled=True)]
    scatter x1 -> x0, local copies, waits for them, and re-layouts: 15.5 us -> none  [secular_roots(): position = jnp.zeros((full_order,), jnp.int32).at[ordering].set(jnp.arang...]
  transfers between devices with their start and end apart: 0 -> 6, of which waited for: 0 -> 4; matrix products, arithmetic and copies ran while one was open for 0% -> 2% of each run, Pallas kernels for 0% -> 0%
where the time goes in v1:
time: 96.9 us; the launch traced here: 95.7 us
  blocking collectives  28.2 us (29%)
  waiting for transfers between devices  23.9 us (25%)
  starting transfers between devices  21.4 us (22%)
  Pallas kernels  18.1 us (19%)
  local copies, waits for them, and re-layouts  1.77 us (2%)
  between operations  1.33 us (1%)
    all_to_all x1, blocking collectives, local(): returned = lax.all_to_all(produced, 'z', 0, 0, tiled=True)  28.2 us
    all_to_all x1, starting transfers between devices, local(): edges = lax.all_to_all(edge, ('z', 'x'), 0, 0, tiled=True)  11.7 us
    pallas_call x1, Pallas kernels, local(): pl.pallas_call(vectors_kernel, grid=(nz // per,), out_shape=jax.ShapeDtyp...  11 us
    ppermute x1, waiting for transfers between devices, local(): lax.ppermute(right[1], 'x', back)  8.49 us
    all_to_all x1, waiting for transfers between devices, local(): edges = lax.all_to_all(edge, ('z', 'x'), 0, 0, tiled=True)  8.13 us
    pallas_call x1, Pallas kernels, local(): pl.pallas_call(roots_kernel, out_shape=(jax.ShapeDtypeStruct((group, bloc...  7.1 us
    all_to_all x1, waiting for transfers between devices, local(): parts = lax.all_to_all(parts, ('z', 'x'), 0, 0, tiled=True)  6.04 us
    all_to_all x1, starting transfers between devices, local(): parts = lax.all_to_all(parts, ('z', 'x'), 0, 0, tiled=True)  5.47 us
  transfers between devices with their start and end apart: 6, of which 4 were waited for; matrix products, arithmetic and copies ran while one was open for 2% of the time, Pallas kernels for 0%

profile of v1, /device:TPU:26, one launch (start us, length us, event | category | flops | bytes accessed | tf_op | source)
XLA Modules:
  0.0 95.7 jit_solution(8657703471902778063)
XLA Ops:
  0.6 1.6 %collective-permute-start = (bf16[2,64,2048]{2,1,0:T(8,128)(2,1)}, bf16[2,64,2048]{2,1,0:T(8,128)(2,1)S(1)}, u32[]{:S(2)}, u32[]{:S(2)}) collective-permute-start(bf16[2,64,2048]{2,1,0:T(8,128)(2,1)} %own.1), channel_id=1, source_target_pairs={{0,1},{1,2},{2,3},{3,0},{4,5},{5,6},{6,7},{7,4},{8,9},{9,10},{10,1... | collective-permute-start | bytes 1572872 | tf_op jit(solution)/shard_map/ppermute | solution.py:185
  2.2 0.5 collective-permute-start.1
  2.7 0.8 fusion
  3.6 0.7 broadcast_in_dim.2
  4.2 0.0 copy-start.1
  4.2 0.0 copy-start.2
  4.2 11.7 %all-to-all-start = ((bf16[32,16,128]{2,1,0:T(8,128)(2,1)}), bf16[32,16,128]{2,1,0:T(8,128)(2,1)S(1)}, u32[]{:S(2)}, u32[]{:S(2)}) async-start(bf16[32,16,128]{2,1,0:T(8,128)(2,1)} %broadcast_in_dim.2), calls=%async_computation | async-start | bytes 262144 | tf_op jit(solution)/shard_map/all_to_all | solution.py:191
  16.6 0.1 pad_add_fusion.place
  16.7 0.0 collective-permute-done.left
  16.7 0.0 collective-permute-done.1.right
  16.7 8.1 %all-to-all-done.edges = bf16[32,16,128]{2,1,0:T(8,128)(2,1)S(1)} async-done(((bf16[32,16,128]{2,1,0:T(8,128)(2,1)}), bf16[32,16,128]{2,1,0:T(8,128)(2,1)S(1)}, u32[]{:S(2)}, u32[]{:S(2)}) %all-to-all-start) | async-done | bytes 131104 | tf_op jit(solution)/shard_map/all_to_all | solution.py:191
  24.9 0.0 copy-done.1
  24.9 0.0 copy-done.2
  24.9 7.1 %roots.1 = (f32[32,40,128]{2,1,0:T(8,128)}, f32[1,128]{1,0:T(1,128)}, f32[1,4096]{1,0:T(1,128)S(1)}) custom-call(s32[2]{0:T(128)S(1)} %pad_add_fusion.place, f32[1]{0:T(128)S(6)} %copy.7.rho_ref, bf16[32,16,128]{2,1,0:T(8,128)(2,1)S(1)} %all-to-all-done.edges, f32[1,4096]{1,0:T(1,128)S(1)} %bitcast.12, s32[1,4096]{1,0:T(1,128)S(1)} %bitcast.14), custom_call_target="tpu_custom_call" | custom-call | tf_op jit(solution)/shard_map/roots/pallas_call | solution.py:196
  32.0 5.5 %all-to-all-start.1 = ((f32[32,40,128]{2,1,0:T(8,128)}), f32[32,40,128]{2,1,0:T(8,128)S(1)}, u32[]{:S(2)}, u32[]{:S(2)}) async-start(f32[32,40,128]{2,1,0:T(8,128)} %get-tuple-element.10), calls=%async_computation.1 | async-start | bytes 1310720 | tf_op jit(solution)/shard_map/all_to_all | solution.py:214
  37.4 0.0 copy-start
  37.5 0.4 collective-permute-start.3
  37.9 1.7 %collective-permute-start.2 = (bf16[64,2048]{1,0:T(8,128)(2,1)S(1)}, bf16[64,2048]{1,0:T(8,128)(2,1)S(1)}, u32[]{:S(2)}, u32[]{:S(2)}) collective-permute-start(bf16[64,2048]{1,0:T(8,128)(2,1)S(1)} %slice_bitcast_fusion.1), channel_id=1, source_target_pairs={{0,1},{1,2},{2,3},{3,0},{4,5},{5,6},{6,7},{7,4},{8,9},{9,10},{10,1... | collective-permute-start | bytes 786440 | tf_op jit(solution)/shard_map/ppermute | solution.py:193
  39.6 8.5 %collective-permute-done.3.far1 = bf16[64,2048]{1,0:T(8,128)(2,1)S(1)} collective-permute-done((bf16[64,2048]{1,0:T(8,128)(2,1)S(1)}, bf16[64,2048]{1,0:T(8,128)(2,1)S(1)}, u32[]{:S(2)}, u32[]{:S(2)}) %collective-permute-start.3) | collective-permute-done | bytes 262176 | tf_op jit(solution)/shard_map/ppermute | solution.py:193
  48.1 1.3 %collective-permute-done.2.far0 = bf16[64,2048]{1,0:T(8,128)(2,1)S(1)} collective-permute-done((bf16[64,2048]{1,0:T(8,128)(2,1)S(1)}, bf16[64,2048]{1,0:T(8,128)(2,1)S(1)}, u32[]{:S(2)}, u32[]{:S(2)}) %collective-permute-start.2) | collective-permute-done | bytes 262176 | tf_op jit(solution)/shard_map/ppermute | solution.py:193
  49.4 6.0 %all-to-all-done.1.parts = f32[32,40,128]{2,1,0:T(8,128)S(1)} async-done(((f32[32,40,128]{2,1,0:T(8,128)}), f32[32,40,128]{2,1,0:T(8,128)S(1)}, u32[]{:S(2)}, u32[]{:S(2)}) %all-to-all-start.1) | async-done | bytes 655392 | tf_op jit(solution)/shard_map/all_to_all | solution.py:214
  55.4 0.0 copy-done
  55.4 11.0 %vectors.1 = bf16[8,2,256,128]{3,2,1,0:T(8,128)(2,1)S(1)} custom-call(s32[2]{0:T(128)S(1)} %pad_add_fusion.place, f32[1]{0:T(128)S(6)} %copy.7.rho_ref, f32[32,40,128]{2,1,0:T(8,128)S(1)} %all-to-all-done.1.parts, f32[1,4096]{1,0:T(1,128)S(1)} %bitcast.13, s32[1,4096]{1,0:T(1,128)S(1)} %bitcast.15, f32[1,4096]{1,0:T(1,128)S(1)} %get-tuple-element.11.zrow, ...), custom_call_target="tpu_custom_call" | custom-call | tf_op jit(solution)/shard_map/vectors/pallas_call | solution.py:216
  66.5 28.2 %all_to_all.15 = bf16[8,2,256,128]{3,2,1,0:T(8,128)(2,1)S(1)} all-to-all(bf16[8,2,256,128]{3,2,1,0:T(8,128)(2,1)S(1)} %vectors.1), channel_id=1, replica_groups=mesh['merge'=8,'z'=8,'x'=4] {'z'}, dimensions={0} | all-to-all | bytes 2097152 | tf_op jit(solution)/shard_map/all_to_all | solution.py:233
  94.7 1.0 %copy.6 = bf16[2,8,256,128]{3,2,1,0:T(8,128)(2,1)} copy(bf16[2,8,256,128]{3,2,0,1:T(8,128)(2,1)S(1)} %bitcast.16) | data formatting | bytes 2097152 | tf_op jit(solution)/shard_map/transpose | solution.py:234
  (2 shorter events, 0.0 us)
Async XLA Ops:
  0.6 16.1 %collective-permute-start = (bf16[2,64,2048]{2,1,0:T(8,128)(2,1)}, bf16[2,64,2048]{2,1,0:T(8,128)(2,1)S(1)}, u32[]{:S(2)}, u32[]{:S(2)}) collective-permute-start(bf16[2,64,2048]{2,1,0:T(8,128)(2,1)} %own.1), channel_id=1, source_target_pairs={{0,1},{1,2},{2,3},{3,0},{4,5},{5,6},{6,7},{7,4},{8,9},{9,10},{10,1... | collective-permute-start | bytes 1572872 | tf_op jit(solution)/shard_map/ppermute | solution.py:185
  2.2 14.5 %collective-permute-start.1 = (bf16[2,64,2048]{2,1,0:T(8,128)(2,1)}, bf16[2,64,2048]{2,1,0:T(8,128)(2,1)S(1)}, u32[]{:S(2)}, u32[]{:S(2)}) collective-permute-start(bf16[2,64,2048]{2,1,0:T(8,128)(2,1)} %own.1), channel_id=1, source_target_pairs={{0,3},{1,0},{2,1},{3,2},{4,7},{5,4},{6,5},{7,6},{8,11},{9,8},{10,9... | collective-permute-start | bytes 1572872 | tf_op jit(solution)/shard_map/ppermute | solution.py:186
  4.2 20.6 %copy-start.1 = (f32[4096]{0:T(1024)S(1)}, f32[4096]{0:T(1024)}, u32[]{:S(2)}) copy-start(f32[4096]{0:T(1024)} %param.6) | copy-start | bytes 49156
  4.2 20.6 %copy-start.2 = (s32[4096]{0:T(1024)S(1)}, s32[4096]{0:T(1024)}, u32[]{:S(2)}) copy-start(s32[4096]{0:T(1024)} %param.7) | copy-start | bytes 49156
  4.2 20.6 %all-to-all-start = ((bf16[32,16,128]{2,1,0:T(8,128)(2,1)}), bf16[32,16,128]{2,1,0:T(8,128)(2,1)S(1)}, u32[]{:S(2)}, u32[]{:S(2)}) async-start(bf16[32,16,128]{2,1,0:T(8,128)(2,1)} %broadcast_in_dim.2), calls=%async_computation | async-start | bytes 262144 | tf_op jit(solution)/shard_map/all_to_all | solution.py:191
  32.0 23.4 %all-to-all-start.1 = ((f32[32,40,128]{2,1,0:T(8,128)}), f32[32,40,128]{2,1,0:T(8,128)S(1)}, u32[]{:S(2)}, u32[]{:S(2)}) async-start(f32[32,40,128]{2,1,0:T(8,128)} %get-tuple-element.10), calls=%async_computation.1 | async-start | bytes 1310720 | tf_op jit(solution)/shard_map/all_to_all | solution.py:214
  37.4 18.0 %copy-start = (bf16[2,64,2048]{2,1,0:T(8,128)(2,1)S(1)}, bf16[2,64,2048]{2,1,0:T(8,128)(2,1)}, u32[]{:S(2)}) copy-start(bf16[2,64,2048]{2,1,0:T(8,128)(2,1)} %own.1) | copy-start | bytes 1572868
  37.5 10.6 %collective-permute-start.3 = (bf16[64,2048]{1,0:T(8,128)(2,1)S(1)}, bf16[64,2048]{1,0:T(8,128)(2,1)S(1)}, u32[]{:S(2)}, u32[]{:S(2)}) collective-permute-start(bf16[64,2048]{1,0:T(8,128)(2,1)S(1)} %slice_bitcast_fusion), channel_id=1, source_target_pairs={{0,3},{1,0},{2,1},{3,2},{4,7},{5,4},{6,5},{7,6},{8,11},{9,8},{10,9... | collective-permute-start | bytes 786440 | tf_op jit(solution)/shard_map/ppermute | solution.py:193
  37.9 11.4 %collective-permute-start.2 = (bf16[64,2048]{1,0:T(8,128)(2,1)S(1)}, bf16[64,2048]{1,0:T(8,128)(2,1)S(1)}, u32[]{:S(2)}, u32[]{:S(2)}) collective-permute-start(bf16[64,2048]{1,0:T(8,128)(2,1)S(1)} %slice_bitcast_fusion.1), channel_id=1, source_target_pairs={{0,1},{1,2},{2,3},{3,0},{4,5},{5,6},{6,7},{7,4},{8,9},{9,10},{10,1... | collective-permute-start | bytes 786440 | tf_op jit(solution)/shard_map/ppermute | solution.py:193

commit v2 on v1

v2 whole, which is shorter than its diff:
```python
import functools

import jax
import jax.numpy as jnp
from jax import lax
from jax.experimental import pallas as pl
from jax.experimental.pallas import tpu as pltpu
from jax.sharding import Mesh, PartitionSpec as P

ITERS = 4
MARGIN = 0.05
FAR = 1.0e6
LANES = 128


def column_of(row):
    n = row.shape[1]
    eye = lax.broadcasted_iota(jnp.int32, (n, n), 0) == lax.broadcasted_iota(jnp.int32, (n, n), 1)
    return jnp.sum(jnp.where(eye, row, 0.0), axis=1, keepdims=True)


def row_of(column):
    n = column.shape[0]
    eye = lax.broadcasted_iota(jnp.int32, (n, n), 0) == lax.broadcasted_iota(jnp.int32, (n, n), 1)
    return jnp.sum(jnp.where(eye, column, 0.0), axis=0, keepdims=True)


def roots_kernel(place, rho_ref, edges, values, flags, out, eig, zrow_out, far, weight, dist, pdi, pde, prod):
    member = place[0]
    rho = rho_ref[0]
    full = values.shape[1]
    blocks = full // LANES
    half_rows = blocks // 2
    last = edges.shape[0] - 1
    halves = (edges[last].astype(jnp.float32), edges[0].astype(jnp.float32))
    for b in range(blocks):
        zrow_out[:, b * LANES : (b + 1) * LANES] = halves[b // half_rows][b % half_rows : b % half_rows + 1, :]
    live = flags[...] == 0
    z = jnp.where(live, zrow_out[...], 0.0)
    zrow_out[...] = z
    total = rho * jnp.sum(z * z)
    weight[...] = jnp.broadcast_to(z * z, weight.shape)
    far[...] = jnp.broadcast_to(jnp.where(live, values[...], FAR), far.shape)
    own = pl.ds(pl.multiple_of(member * LANES, LANES), LANES)
    own_values = values[:, own]
    own_live = flags[:, own] == 0
    pdi[...] = jnp.broadcast_to(column_of(own_values), (LANES, LANES))
    inv_rho = 1.0 / rho
    depth = 8
    tiles = LANES // 8

    def spread(column):
        return jnp.broadcast_to(column, (8, LANES))

    gap = []
    for g in range(0, tiles, depth):
        di = [pdi[8 * (g + r) : 8 * (g + r) + 8, :] for r in range(depth)]
        low = [jnp.full((8, LANES), 2.0 * FAR, jnp.float32) for _ in range(depth)]
        for b in range(blocks):
            sl = slice(b * LANES, (b + 1) * LANES)
            d = far[:, sl]
            for r in range(depth):
                e = d - di[r]
                dist[8 * (g + r) : 8 * (g + r) + 8, sl] = e
                low[r] = jnp.minimum(low[r], jnp.where(e > 0, e, 2.0 * FAR))
        for r in range(depth):
            least = spread(jnp.min(low[r], axis=1, keepdims=True))
            gap.append(jnp.where(least > 0.5 * FAR, (di[r] + total) - di[r], least))
    for r in range(tiles):
        pdi[8 * r : 8 * r + 8, :] = gap[r]
        pde[8 * r : 8 * r + 8, :] = 0.5 * gap[r]

    def sweep(_, carry):
        for g in range(0, tiles, depth):
            de = [pde[8 * (g + r) : 8 * (g + r) + 8, :] for r in range(depth)]
            f = [jnp.zeros((8, LANES), jnp.float32) for _ in range(depth)]
            h = [jnp.zeros((8, LANES), jnp.float32) for _ in range(depth)]
            for b in range(blocks):
                sl = slice(b * LANES, (b + 1) * LANES)
                w = weight[:, sl]
                for r in range(depth):
                    inverse = pltpu.reciprocal(dist[8 * (g + r) : 8 * (g + r) + 8, sl] - de[r], approx=True)
                    term = w * inverse
                    f[r] = f[r] + term
                    h[r] = h[r] + term * inverse
            for r in range(depth):
                top = inv_rho + spread(jnp.sum(f[r], axis=1, keepdims=True))
                slope = spread(jnp.sum(h[r], axis=1, keepdims=True))
                gp = pdi[8 * (g + r) : 8 * (g + r) + 8, :]
                pde[8 * (g + r) : 8 * (g + r) + 8, :] = jnp.clip(de[r] - top / slope, MARGIN * gp, (1.0 - MARGIN) * gp)
        return carry

    lax.fori_loop(0, ITERS, sweep, 0, unroll=True)
    own_delta = jnp.where(own_live, row_of(pde[...][:, :1]), 0.0)
    eig[...] = own_values + own_delta
    pde[...] = jnp.broadcast_to(column_of(own_delta), (LANES, LANES))
    for b in range(blocks):
        sl = slice(b * LANES, (b + 1) * LANES)
        p = None
        for g in range(0, tiles, 4):
            num = den = None
            for r in range(g, g + 4):
                e = dist[8 * r : 8 * r + 8, sl]
                a = e - pde[8 * r : 8 * r + 8, :]
                c = jnp.where(e == 0, 1.0, e)
                num = a if num is None else num * a
                den = c if den is None else den * c
            ratio = num * pltpu.reciprocal(den, approx=True)
            p = ratio if p is None else p * ratio
        prod[:, sl] = p
    p = prod[...]
    p = p[:4] * p[4:]
    p = p[:2] * p[2:]
    p = p[:1] * p[1:]
    for b in range(blocks):
        out[b : b + 1, :] = p[:, b * LANES : (b + 1) * LANES]
    out[blocks : blocks + 1, :] = own_delta
    out[blocks + 1 :, :] = jnp.zeros((out.shape[0] - blocks - 1, LANES), jnp.float32)


def vectors_kernel(offsets, place, rho_ref, parts, values, flags, *refs):
    first = len(refs) == 14
    if first:
        zrow, own, left, right, far0, far1, *outs, zhat, far = refs[:-4]
    else:
        zhat, far, own, left, right, far0, far1, *outs = refs[:-4]
    basis, held, pdi, pde = refs[-4:]
    z, x = place[1], place[2]
    nz, nx = 8, 4
    share = own.shape[1]
    full = values.shape[1]
    half = full // 2
    blocks = full // LANES

    if first:
        p = parts[0, :blocks]
        for s in range(1, parts.shape[0]):
            p = p * parts[s, :blocks]
        p = jnp.sqrt(jnp.abs(p) / rho_ref[0])
        for r in range(blocks):
            zhat[:, r * LANES : (r + 1) * LANES] = jnp.broadcast_to(p[r : r + 1, :], (8, LANES))
        live = flags[...] == 0
        live8 = jnp.broadcast_to(flags[...], far.shape) == 0
        signed = jnp.where(jnp.broadcast_to(zrow[...], far.shape) >= 0, zhat[...], -zhat[...])
        zhat[...] = jnp.where(live8, signed, 0.0)
        far[...] = jnp.broadcast_to(jnp.where(live, values[...], FAR), far.shape)

    places = [lax.rem(z + offset, nz) for offset in offsets]
    owners = [at * nx + x for at in places]
    for k, owner in enumerate(owners):
        cols = pl.ds(pl.multiple_of(owner * LANES, LANES), LANES)
        pdi[k * LANES : (k + 1) * LANES, :] = jnp.broadcast_to(column_of(values[:, cols]), (LANES, LANES))
        pde[k * LANES : (k + 1) * LANES, :] = jnp.broadcast_to(
            column_of(parts[places[k], blocks : blocks + 1, :]), (LANES, LANES)
        )
    depth = 8

    def group(g):
        base = g * 8 * depth
        di = [pdi[pl.ds(base + 8 * r, 8), :] for r in range(depth)]
        de = [pde[pl.ds(base + 8 * r, 8), :] for r in range(depth)]
        acc = [jnp.zeros((8, LANES), jnp.float32) for _ in range(depth)]
        for b in range(blocks):
            sl = slice(b * LANES, (b + 1) * LANES)
            d, zh = far[:, sl], zhat[:, sl]
            for r in range(depth):
                v = zh * pltpu.reciprocal((d - di[r]) - de[r], approx=True)
                acc[r] = acc[r] + v * v
                held[8 * r : 8 * r + 8, sl] = v
        scale = [lax.rsqrt(jnp.sum(a, axis=1, keepdims=True)) for a in acc]
        scale = [jnp.broadcast_to(a, (8, LANES)) for a in scale]
        for b in range(blocks):
            sl = slice(b * LANES, (b + 1) * LANES)
            for r in range(0, depth, 2):
                u = [held[8 * t : 8 * t + 8, sl] * scale[t] for t in (r, r + 1)]
                basis[pl.ds(base + 8 * r, 16), sl] = jnp.concatenate(u, axis=0).astype(jnp.bfloat16)

    for g in range(len(offsets) * LANES // (8 * depth)):
        group(g)
    for c in range(2):
        slots = (own.at[c], left.at[c], right.at[c], (far0, far1)[c])
        lhs = jnp.concatenate([slot[...] for slot in slots], axis=0)
        rhs = basis[:, c * half : (c + 1) * half]
        acc = lax.dot_general(lhs, rhs, (((1,), (1,)), ((), ())), preferred_element_type=jnp.float32)
        for k, owner in enumerate(owners):
            dead = flags[:, pl.ds(pl.multiple_of(owner * LANES, LANES), LANES)] != 0
            mine = owner < blocks // 2 if c == 0 else owner >= blocks // 2
            inner = jnp.where(mine, owner if c == 0 else owner - blocks // 2, 0)
            for s, slot in enumerate(slots):
                plain = slot[:, pl.ds(pl.multiple_of(inner * LANES, LANES), LANES)].astype(jnp.float32)
                plain = jnp.where(mine, plain, 0.0)
                got = acc[s * share : (s + 1) * share, k * LANES : (k + 1) * LANES]
                source = lax.rem(x + (0, nx - 1, 1, 2)[s], nx)
                outs[k][c, pl.ds(pl.multiple_of(source * share, share), share), :] = jnp.where(dead, plain, got).astype(
                    jnp.bfloat16
                )


def assemble_kernel(order, place, *refs):
    pieces, out, sems = refs[:-2], refs[-2], refs[-1]
    nz = len(pieces)
    copies = []
    for k, (offset, piece) in enumerate(zip(order, pieces)):
        source = lax.rem(place[1] + nz - offset, nz)
        copy = pltpu.make_async_copy(piece, out.at[:, source], sems.at[k])
        copy.start()
        copies.append(copy)
    for copy in copies:
        copy.wait()


def local(child_vectors, child_values, deflated, order, coupling):
    del order
    half = child_vectors.shape[2]
    full = 2 * half
    rows = child_vectors.shape[1]
    nz, nx = lax.axis_size("z"), lax.axis_size("x")
    group = nz * nx
    z, x = lax.axis_index("z"), lax.axis_index("x")
    member = z * nx + x
    blocks = full // LANES
    whole = lambda: pl.BlockSpec(memory_space=pltpu.VMEM)
    scalar = lambda: pl.BlockSpec(memory_space=pltpu.SMEM)

    ahead = [(i, (i + 1) % nx) for i in range(nx)]
    back = [(i, (i - 1) % nx) for i in range(nx)]
    left = lax.ppermute(child_vectors, "x", ahead)
    right = lax.ppermute(child_vectors, "x", back)

    place = jnp.stack([member, z, x]).astype(jnp.int32)
    edge = jnp.where(member == group - 1, child_vectors[0, rows - 1], child_vectors[1, 0])
    edge = jnp.broadcast_to(edge.reshape(1, half // LANES, LANES), (group, half // LANES, LANES))
    edges = lax.all_to_all(edge, ("z", "x"), 0, 0, tiled=True)
    child_values, left, right = lax.optimization_barrier((child_values, left, right))
    values = child_values.reshape(1, full)
    flags = deflated.reshape(1, full)
    block, eig, zrow = pl.pallas_call(
        roots_kernel,
        out_shape=(
            jax.ShapeDtypeStruct((blocks + 8, LANES), jnp.float32),
            jax.ShapeDtypeStruct((1, LANES), jnp.float32),
            jax.ShapeDtypeStruct((1, full), jnp.float32),
        ),
        in_specs=[scalar(), scalar(), whole(), whole(), whole()],
        out_specs=(whole(), whole(), whole()),
        scratch_shapes=[
            pltpu.VMEM((8, full), jnp.float32),
            pltpu.VMEM((8, full), jnp.float32),
            pltpu.VMEM((LANES, full), jnp.float32),
            pltpu.VMEM((LANES, LANES), jnp.float32),
            pltpu.VMEM((LANES, LANES), jnp.float32),
            pltpu.VMEM((8, full), jnp.float32),
        ],
        compiler_params=pltpu.CompilerParams(vmem_limit_bytes=32 * 1024 * 1024),
        name="roots",
    )(place, coupling, edges, values, flags)
    others = [lax.ppermute(block, "x", [(i, (i + k) % nx) for i in range(nx)]) for k in (2, 1, 3)]
    left, right, *others = lax.optimization_barrier((left, right, *others))
    opposite = (lax.ppermute(left[0], "x", ahead), lax.ppermute(right[1], "x", back))
    product = block
    for other in others:
        product = product * other
    lines = lax.broadcasted_iota(jnp.int32, block.shape, 0)
    parts = jnp.broadcast_to(jnp.where(lines < blocks, product, block), (nz,) + block.shape)
    parts = lax.all_to_all(parts, "z", 0, 0, tiled=True)
    order = (4, 5, 3, 6, 2, 7, 1, 0)
    piece = jax.ShapeDtypeStruct((2, nx * rows, LANES), jnp.bfloat16)
    wide = jax.ShapeDtypeStruct((8, full), jnp.float32)
    held = (zrow,)
    pieces = []
    for at in range(0, nz, 2):
        pair = order[at : at + 2]
        extra = (wide, wide) if at == 0 else ()
        *made, = pl.pallas_call(
            functools.partial(vectors_kernel, pair),
            out_shape=(piece,) * 2 + extra,
            in_specs=[scalar(), scalar()] + [whole()] * (8 + len(held)),
            out_specs=(whole(),) * (2 + len(extra)),
            scratch_shapes=[
                pltpu.VMEM((2 * LANES, full), jnp.bfloat16),
                pltpu.VMEM((64, full), jnp.float32),
                pltpu.VMEM((2 * LANES, LANES), jnp.float32),
                pltpu.VMEM((2 * LANES, LANES), jnp.float32),
            ],
            compiler_params=pltpu.CompilerParams(vmem_limit_bytes=24 * 1024 * 1024),
            name="vectors",
        )(place, coupling, parts, values, flags, *held, child_vectors, left, right, *opposite)
        if at == 0:
            held = tuple(made[2:])
        for offset, block in zip(pair, made[:2]):
            if offset:
                block = lax.ppermute(block, "z", [(i, (i + offset) % nz) for i in range(nz)])
            pieces.append(block)
    eigenvectors = pl.pallas_call(
        functools.partial(assemble_kernel, order),
        out_shape=jax.ShapeDtypeStruct((2, nz, nx * rows, LANES), jnp.bfloat16),
        in_specs=[scalar()] + [whole()] * nz,
        out_specs=pl.BlockSpec(memory_space=pl.ANY),
        scratch_shapes=[pltpu.SemaphoreType.DMA((nz,))],
        name="assemble",
    )(place, *pieces).reshape(full, LANES)
    return eig.reshape(LANES), eigenvectors


def solution(mesh):
    inner = Mesh(mesh.devices.reshape(mesh.devices.shape[0], -1, 4), ("merge", "z", "x"))
    grp = ("z", "x")
    in_specs = (P("merge", grp, None), P("merge"), P("merge"), P("merge"), P("merge"))
    out_specs = (P(("merge",) + grp), P("merge", grp))
    return jax.shard_map(local, mesh=inner, in_specs=in_specs, out_specs=out_specs, check_vma=False)
```

time: 96.9 us -> 84.3 us (0.87)
  blocking collectives: 28.2 us -> 0 us
  starting transfers between devices: 21.4 us -> 38.2 us
  Pallas kernels: 18.1 us -> 15.5 us
    all_to_all x1 -> x0, blocking collectives: 28.2 us -> none  [local(): returned = lax.all_to_all(produced, 'z', 0, 0, tiled=True)]
    ppermute x0 -> x10, starting transfers between devices: none -> 18.8 us  [the longest x7 14.6 us: local(): lax.ppermute(block, 'z', [(i, (i + offset) % nz) for i in range(nz)])]
    ppermute x0 -> x10, waiting for transfers between devices: none -> 9.14 us  [the longest x7 6.14 us: local(): lax.ppermute(block, 'z', [(i, (i + offset) % nz) for i in range(nz)])]
    ppermute x1, waiting for transfers between devices: 8.49 us -> 1.66 us  [local(): lax.ppermute(right[1], 'x', back)]
    all_to_all x1, waiting for transfers between devices: 6.04 us -> 1.2 us  [local(): parts = lax.all_to_all(parts, 'z', 0, 0, tiled=True)]
    ppermute x1, waiting for transfers between devices: 1.28 us -> 4.25 us  [local(): lax.ppermute(left[0], 'x', ahead)]
    pallas_call x2 -> x6, Pallas kernels: 18.1 us -> 15.5 us  [the longest x4 9.52 us: local(): pl.pallas_call(functools.partial(vectors_kernel, pair), out_shape=(piece,...]
    all_to_all x1, starting transfers between devices: 5.47 us -> 3.38 us  [local(): parts = lax.all_to_all(parts, 'z', 0, 0, tiled=True)]
  transfers between devices with their start and end apart: 6 -> 16, of which waited for: 4 -> 9; matrix products, arithmetic and copies ran while one was open for 2% -> 2% of each run, Pallas kernels for 0% -> 9%
where the time goes in v2:
time: 84.3 us; the launch traced here: 83.4 us
  starting transfers between devices  38.2 us (45%)
  waiting for transfers between devices  24.4 us (29%)
  Pallas kernels  15.5 us (18%)
  local copies, waits for them, and re-layouts  2.71 us (3%)
  between operations  1.6 us (2%)
  other arithmetic  0.99 us (1%)
    ppermute x7, starting transfers between devices, local(): lax.ppermute(block, 'z', [(i, (i + offset) % nz) for i in range(nz)])  14.6 us
    all_to_all x1, starting transfers between devices, local(): edges = lax.all_to_all(edge, ('z', 'x'), 0, 0, tiled=True)  11.7 us
    pallas_call x4, Pallas kernels, local(): pl.pallas_call(functools.partial(vectors_kernel, pair), out_shape=(piece,...  9.52 us
    all_to_all x1, waiting for transfers between devices, local(): edges = lax.all_to_all(edge, ('z', 'x'), 0, 0, tiled=True)  8.12 us
    ppermute x7, waiting for transfers between devices, local(): lax.ppermute(block, 'z', [(i, (i + offset) % nz) for i in range(nz)])  6.14 us
    ppermute x1, waiting for transfers between devices, local(): lax.ppermute(left[0], 'x', ahead)  4.25 us
    ppermute x3, starting transfers between devices, local(): lax.ppermute(block, 'x', [(i, (i + k) % nx) for i in range(nx)])  4.15 us
    pallas_call x1, Pallas kernels, local(): pl.pallas_call(roots_kernel, out_shape=(jax.ShapeDtypeStruct((blocks + 8,...  3.68 us
  transfers between devices with their start and end apart: 16, of which 9 were waited for; matrix products, arithmetic and copies ran while one was open for 2% of the time, Pallas kernels for 9%

profile of v2, /device:TPU:26, one launch (start us, length us, event | category | flops | bytes accessed | tf_op | source)
XLA Modules:
  0.0 83.4 jit_solution(2172615302213083084)
XLA Ops:
  0.6 1.6 %collective-permute-start = (bf16[2,64,2048]{2,1,0:T(8,128)(2,1)}, bf16[2,64,2048]{2,1,0:T(8,128)(2,1)S(1)}, u32[]{:S(2)}, u32[]{:S(2)}) collective-permute-start(bf16[2,64,2048]{2,1,0:T(8,128)(2,1)} %refs_2_.5), channel_id=1, source_target_pairs={{0,1},{1,2},{2,3},{3,0},{4,5},{5,6},{6,7},{7,4},{8,9},{9,10},{10,1... | collective-permute-start | bytes 1572872 | tf_op jit(solution)/shard_map/ppermute | solution.py:227
  2.7 0.8 fusion
  3.6 0.7 broadcast_in_dim.8
  4.2 11.7 %all-to-all-start = ((bf16[32,16,128]{2,1,0:T(8,128)(2,1)}), bf16[32,16,128]{2,1,0:T(8,128)(2,1)S(1)}, u32[]{:S(2)}, u32[]{:S(2)}) async-start(bf16[32,16,128]{2,1,0:T(8,128)(2,1)} %broadcast_in_dim.8), calls=%async_computation | async-start | bytes 262144 | tf_op jit(solution)/shard_map/all_to_all | solution.py:233
  16.7 8.1 %all-to-all-done.edges = bf16[32,16,128]{2,1,0:T(8,128)(2,1)S(1)} async-done(((bf16[32,16,128]{2,1,0:T(8,128)(2,1)}), bf16[32,16,128]{2,1,0:T(8,128)(2,1)S(1)}, u32[]{:S(2)}, u32[]{:S(2)}) %all-to-all-start) | async-done | bytes 131104 | tf_op jit(solution)/shard_map/all_to_all | solution.py:233
  24.9 3.7 %roots.1 = (f32[40,128]{1,0:T(8,128)S(1)}, f32[1,128]{1,0:T(1,128)}, f32[1,4096]{1,0:T(1,128)S(1)}) custom-call(s32[3]{0:T(128)S(1)} %pad_add_fusion.place, f32[1]{0:T(128)S(6)} %copy.6.rho_ref, bf16[32,16,128]{2,1,0:T(8,128)(2,1)S(1)} %all-to-all-done.edges, f32[1,4096]{1,0:T(1,128)S(1)} %bitcast.12, s32[1,4096]{1,0:T(1,128)S(1)} %bitcast.17), custom_call_target="tpu_custom_call" | custom-call | tf_op jit(solution)/shard_map/roots/pallas_call | solution.py:237
  28.5 2.1 %collective-permute-start.2 = (f32[40,128]{1,0:T(8,128)S(1)}, f32[40,128]{1,0:T(8,128)S(1)}, u32[]{:S(2)}, u32[]{:S(2)}) collective-permute-start(f32[40,128]{1,0:T(8,128)S(1)} %get-tuple-element.25), channel_id=1, source_target_pairs={{0,2},{1,3},{2,0},{3,1},{4,6},{5,7},{6,4},{7,5},{8,10},{9,11},{10,... | collective-permute-start | bytes 61448 | tf_op jit(solution)/shard_map/ppermute | solution.py:257
  30.7 1.3 %collective-permute-start.3 = (f32[40,128]{1,0:T(8,128)S(1)}, f32[40,128]{1,0:T(8,128)S(1)}, u32[]{:S(2)}, u32[]{:S(2)}) collective-permute-start(f32[40,128]{1,0:T(8,128)S(1)} %get-tuple-element.25), channel_id=1, source_target_pairs={{0,1},{1,2},{2,3},{3,0},{4,5},{5,6},{6,7},{7,4},{8,9},{9,10},{10,1... | collective-permute-start | bytes 61448 | tf_op jit(solution)/shard_map/ppermute | solution.py:257
  31.9 0.8 collective-permute-start.4
  32.7 1.1 %collective-permute-done.2 = f32[40,128]{1,0:T(8,128)S(1)} collective-permute-done((f32[40,128]{1,0:T(8,128)S(1)}, f32[40,128]{1,0:T(8,128)S(1)}, u32[]{:S(2)}, u32[]{:S(2)}) %collective-permute-start.2) | collective-permute-done | bytes 20512 | tf_op jit(solution)/shard_map/ppermute | solution.py:257
  33.8 0.6 collective-permute-done.3
  34.5 1.3 %collective-permute-done.4 = f32[40,128]{1,0:T(8,128)S(1)} collective-permute-done((f32[40,128]{1,0:T(8,128)S(1)}, f32[40,128]{1,0:T(8,128)S(1)}, u32[]{:S(2)}, u32[]{:S(2)}) %collective-permute-start.4) | collective-permute-done | bytes 20512 | tf_op jit(solution)/shard_map/ppermute | solution.py:257
  35.8 0.7 broadcast_in_dim.9
  36.5 3.4 %all-to-all-start.1 = ((f32[8,40,128]{2,1,0:T(8,128)}), f32[8,40,128]{2,1,0:T(8,128)S(1)}, u32[]{:S(2)}, u32[]{:S(2)}) async-start(f32[8,40,128]{2,1,0:T(8,128)} %broadcast_in_dim.9), calls=%async_computation.1 | async-start | bytes 327680 | tf_op jit(solution)/shard_map/all_to_all | solution.py:265
  39.9 0.8 collective-permute-start.5
  40.7 1.4 %collective-permute-start.6 = (bf16[64,2048]{1,0:T(8,128)(2,1)S(1)}, bf16[64,2048]{1,0:T(8,128)(2,1)S(1)}, u32[]{:S(2)}, u32[]{:S(2)}) collective-permute-start(bf16[64,2048]{1,0:T(8,128)(2,1)S(1)} %slice_bitcast_fusion), channel_id=1, source_target_pairs={{0,3},{1,0},{2,1},{3,2},{4,7},{5,4},{6,5},{7,6},{8,11},{9,8},{10,9... | collective-permute-start | bytes 786440 | tf_op jit(solution)/shard_map/ppermute | solution.py:259
  42.1 4.2 %collective-permute-done.5.refs_4_.refs_5_ = bf16[64,2048]{1,0:T(8,128)(2,1)S(1)} collective-permute-done((bf16[64,2048]{1,0:T(8,128)(2,1)S(1)}, bf16[64,2048]{1,0:T(8,128)(2,1)S(1)}, u32[]{:S(2)}, u32[]{:S(2)}) %collective-permute-start.5) | collective-permute-done | bytes 262176 | tf_op jit(solution)/shard_map/ppermute | solution.py:259
  46.3 1.7 %collective-permute-done.6.refs_5_.refs_6_ = bf16[64,2048]{1,0:T(8,128)(2,1)S(1)} collective-permute-done((bf16[64,2048]{1,0:T(8,128)(2,1)S(1)}, bf16[64,2048]{1,0:T(8,128)(2,1)S(1)}, u32[]{:S(2)}, u32[]{:S(2)}) %collective-permute-start.6) | collective-permute-done | bytes 262176 | tf_op jit(solution)/shard_map/ppermute | solution.py:259
  48.0 1.2 %all-to-all-done.1.parts = f32[8,40,128]{2,1,0:T(8,128)S(1)} async-done(((f32[8,40,128]{2,1,0:T(8,128)}), f32[8,40,128]{2,1,0:T(8,128)S(1)}, u32[]{:S(2)}, u32[]{:S(2)}) %all-to-all-start.1) | async-done | bytes 163872 | tf_op jit(solution)/shard_map/all_to_all | solution.py:265
  49.2 2.4 %vectors.4 = (bf16[2,256,128]{2,1,0:T(8,128)(2,1)S(1)}, bf16[2,256,128]{2,1,0:T(8,128)(2,1)S(1)}, f32[8,4096]{1,0:T(8,128)S(1)}, f32[8,4096]{1,0:T(8,128)S(1)}) custom-call(s32[3]{0:T(128)S(1)} %pad_add_fusion.place, f32[1]{0:T(128)S(6)} %copy.6.rho_ref, f32[8,40,128]{2,1,0:T(8,128)S(1)} %all-to-all-done.1.parts, f32[1,4096]{1,0:T(1,128)S(1)} %bitcast.13, ...), custom_call_target="tpu_custom_call" | custom-call | tf_op jit(solution)/shard_map/vectors/pallas_call | solution.py:274
  51.6 4.7 %collective-permute-start.7 = (bf16[2,256,128]{2,1,0:T(8,128)(2,1)S(1)}, bf16[2,256,128]{2,1,0:T(8,128)(2,1)S(1)}, u32[]{:S(2)}, u32[]{:S(2)}) collective-permute-start(bf16[2,256,128]{2,1,0:T(8,128)(2,1)S(1)} %get-tuple-element.34), channel_id=1, source_target_pairs={{0,16},{4,20},{8,24},{12,28},{16,0},{20,4},{24,8},{28,12},{1,17},{... | collective-permute-start | bytes 393224 | tf_op jit(solution)/shard_map/ppermute | solution.py:292
  56.9 2.4 %vectors.5 = (bf16[2,256,128]{2,1,0:T(8,128)(2,1)S(1)}, bf16[2,256,128]{2,1,0:T(8,128)(2,1)S(1)}) custom-call(s32[3]{0:T(128)S(1)} %pad_add_fusion.place, f32[1]{0:T(128)S(6)} %copy.6.rho_ref, f32[8,40,128]{2,1,0:T(8,128)S(1)} %all-to-all-done.1.parts, f32[1,4096]{1,0:T(1,128)S(1)} %bitcast.14, s32[1,4096]{1,0:T(1,128)S(1)} %bitcast.19, ...), custom_call_target="tpu_custom_call" | custom-call | tf_op jit(solution)/shard_map/vectors/pallas_call | solution.py:274
  59.3 3.4 %collective-permute-start.9 = (bf16[2,256,128]{2,1,0:T(8,128)(2,1)S(1)}, bf16[2,256,128]{2,1,0:T(8,128)(2,1)S(1)}, u32[]{:S(2)}, u32[]{:S(2)}) collective-permute-start(bf16[2,256,128]{2,1,0:T(8,128)(2,1)S(1)} %get-tuple-element.38), channel_id=1, source_target_pairs={{0,12},{4,16},{8,20},{12,24},{16,28},{20,0},{24,4},{28,8},{1,13},{... | collective-permute-start | bytes 393224 | tf_op jit(solution)/shard_map/ppermute | solution.py:292
  62.6 1.8 %collective-permute-start.10 = (bf16[2,256,128]{2,1,0:T(8,128)(2,1)S(1)}, bf16[2,256,128]{2,1,0:T(8,128)(2,1)S(1)}, u32[]{:S(2)}, u32[]{:S(2)}) collective-permute-start(bf16[2,256,128]{2,1,0:T(8,128)(2,1)S(1)} %get-tuple-element.39), channel_id=1, source_target_pairs={{0,24},{4,28},{8,0},{12,4},{16,8},{20,12},{24,16},{28,20},{1,25},{... | collective-permute-start | bytes 393224 | tf_op jit(solution)/shard_map/ppermute | solution.py:292
  64.4 2.4 %vectors.6 = (bf16[2,256,128]{2,1,0:T(8,128)(2,1)S(1)}, bf16[2,256,128]{2,1,0:T(8,128)(2,1)S(1)}) custom-call(s32[3]{0:T(128)S(1)} %pad_add_fusion.place, f32[1]{0:T(128)S(6)} %copy.6.rho_ref, f32[8,40,128]{2,1,0:T(8,128)S(1)} %all-to-all-done.1.parts, f32[1,4096]{1,0:T(1,128)S(1)} %bitcast.15, s32[1,4096]{1,0:T(1,128)S(1)} %bitcast.20, ...), custom_call_target="tpu_custom_call" | custom-call | tf_op jit(solution)/shard_map/vectors/pallas_call | solution.py:274
  66.8 1.2 %collective-permute-start.11 = (bf16[2,256,128]{2,1,0:T(8,128)(2,1)S(1)}, bf16[2,256,128]{2,1,0:T(8,128)(2,1)S(1)}, u32[]{:S(2)}, u32[]{:S(2)}) collective-permute-start(bf16[2,256,128]{2,1,0:T(8,128)(2,1)S(1)} %get-tuple-element.40), channel_id=1, source_target_pairs={{0,8},{4,12},{8,16},{12,20},{16,24},{20,28},{24,0},{28,4},{1,9},{5... | collective-permute-start | bytes 393224 | tf_op jit(solution)/shard_map/ppermute | solution.py:292
  68.0 2.4 %vectors.7 = (bf16[2,256,128]{2,1,0:T(8,128)(2,1)S(1)}, bf16[2,256,128]{2,1,0:T(8,128)(2,1)S(1)}) custom-call(s32[3]{0:T(128)S(1)} %pad_add_fusion.place, f32[1]{0:T(128)S(6)} %copy.6.rho_ref, f32[8,40,128]{2,1,0:T(8,128)S(1)} %all-to-all-done.1.parts, f32[1,4096]{1,0:T(1,128)S(1)} %bitcast.16, s32[1,4096]{1,0:T(1,128)S(1)} %bitcast.21, ...), custom_call_target="tpu_custom_call" | custom-call | tf_op jit(solution)/shard_map/vectors/pallas_call | solution.py:274
  70.4 0.7 copy-done.3
  71.1 3.0 %collective-permute-start.12 = (bf16[2,256,128]{2,1,0:T(8,128)(2,1)S(1)}, bf16[2,256,128]{2,1,0:T(8,128)(2,1)S(1)}, u32[]{:S(2)}, u32[]{:S(2)}) collective-permute-start(bf16[2,256,128]{2,1,0:T(8,128)(2,1)S(1)} %get-tuple-element.41), channel_id=1, source_target_pairs={{0,28},{4,0},{8,4},{12,8},{16,12},{20,16},{24,20},{28,24},{1,29},{... | collective-permute-start | bytes 393224 | tf_op jit(solution)/shard_map/ppermute | solution.py:292
  74.1 2.6 %collective-permute-done.11.refs_4_ = bf16[2,256,128]{2,1,0:T(8,128)(2,1)S(1)} collective-permute-done((bf16[2,256,128]{2,1,0:T(8,128)(2,1)S(1)}, bf16[2,256,128]{2,1,0:T(8,128)(2,1)S(1)}, u32[]{:S(2)}, u32[]{:S(2)}) %collective-permute-start.11) | collective-permute-done | bytes 131104 | tf_op jit(solution)/shard_map/ppermute | solution.py:292
  76.7 3.6 %collective-permute-done.13.refs_6_ = bf16[2,256,128]{2,1,0:T(8,128)(2,1)S(1)} collective-permute-done((bf16[2,256,128]{2,1,0:T(8,128)(2,1)S(1)}, bf16[2,256,128]{2,1,0:T(8,128)(2,1)S(1)}, u32[]{:S(2)}, u32[]{:S(2)}) %collective-permute-start.13) | collective-permute-done | bytes 131104 | tf_op jit(solution)/shard_map/ppermute | solution.py:292
  80.9 2.3 %assemble.1 = bf16[2,8,256,128]{3,2,1,0:T(8,128)(2,1)} custom-call(s32[3]{0:T(128)} %copy-done.4, bf16[2,256,128]{2,1,0:T(8,128)(2,1)} %copy-done.5, bf16[2,256,128]{2,1,0:T(8,128)(2,1)} %copy-done.6, bf16[2,256,128]{2,1,0:T(8,128)(2,1)} %copy-done.7, bf16[2,256,128]{2,1,0:T(8,128)(2,1)} %copy-done.8, bf16[2,256,128]{2,1,0:T(8,128)(2,1)} %copy-done.9, ...), custom_call_target="tpu_custom_call" | custom-call | tf_op jit(solution)/shard_map/assemble/pallas_call | solution.py:294
  (38 shorter events, 2.0 us)
Async XLA Ops:
  0.6 16.1 %collective-permute-start = (bf16[2,64,2048]{2,1,0:T(8,128)(2,1)}, bf16[2,64,2048]{2,1,0:T(8,128)(2,1)S(1)}, u32[]{:S(2)}, u32[]{:S(2)}) collective-permute-start(bf16[2,64,2048]{2,1,0:T(8,128)(2,1)} %refs_2_.5), channel_id=1, source_target_pairs={{0,1},{1,2},{2,3},{3,0},{4,5},{5,6},{6,7},{7,4},{8,9},{9,10},{10,1... | collective-permute-start | bytes 1572872 | tf_op jit(solution)/shard_map/ppermute | solution.py:227
  2.2 14.5 %collective-permute-start.1 = (bf16[2,64,2048]{2,1,0:T(8,128)(2,1)}, bf16[2,64,2048]{2,1,0:T(8,128)(2,1)S(1)}, u32[]{:S(2)}, u32[]{:S(2)}) collective-permute-start(bf16[2,64,2048]{2,1,0:T(8,128)(2,1)} %refs_2_.5), channel_id=1, source_target_pairs={{0,3},{1,0},{2,1},{3,2},{4,7},{5,4},{6,5},{7,6},{8,11},{9,8},{10,9... | collective-permute-start | bytes 1572872 | tf_op jit(solution)/shard_map/ppermute | solution.py:228
  4.2 20.6 %copy-start.1 = (f32[4096]{0:T(1024)S(1)}, f32[4096]{0:T(1024)}, u32[]{:S(2)}) copy-start(f32[4096]{0:T(1024)} %param.6) | copy-start | bytes 49156
  4.2 20.6 %copy-start.2 = (s32[4096]{0:T(1024)S(1)}, s32[4096]{0:T(1024)}, u32[]{:S(2)}) copy-start(s32[4096]{0:T(1024)} %param.7) | copy-start | bytes 49156
  4.2 20.6 %all-to-all-start = ((bf16[32,16,128]{2,1,0:T(8,128)(2,1)}), bf16[32,16,128]{2,1,0:T(8,128)(2,1)S(1)}, u32[]{:S(2)}, u32[]{:S(2)}) async-start(bf16[32,16,128]{2,1,0:T(8,128)(2,1)} %broadcast_in_dim.8), calls=%async_computation | async-start | bytes 262144 | tf_op jit(solution)/shard_map/all_to_all | solution.py:233
  16.7 51.3 %copy-start.4 = (s32[3]{0:T(128)}, s32[3]{0:T(128)S(1)}, u32[]{:S(2)}) copy-start(s32[3]{0:T(128)S(1)} %pad_add_fusion.place) | copy-start | bytes 40
  28.5 5.3 %collective-permute-start.2 = (f32[40,128]{1,0:T(8,128)S(1)}, f32[40,128]{1,0:T(8,128)S(1)}, u32[]{:S(2)}, u32[]{:S(2)}) collective-permute-start(f32[40,128]{1,0:T(8,128)S(1)} %get-tuple-element.25), channel_id=1, source_target_pairs={{0,2},{1,3},{2,0},{3,1},{4,6},{5,7},{6,4},{7,5},{8,10},{9,11},{10,... | collective-permute-start | bytes 61448 | tf_op jit(solution)/shard_map/ppermute | solution.py:257
  30.7 3.8 %collective-permute-start.3 = (f32[40,128]{1,0:T(8,128)S(1)}, f32[40,128]{1,0:T(8,128)S(1)}, u32[]{:S(2)}, u32[]{:S(2)}) collective-permute-start(f32[40,128]{1,0:T(8,128)S(1)} %get-tuple-element.25), channel_id=1, source_target_pairs={{0,1},{1,2},{2,3},{3,0},{4,5},{5,6},{6,7},{7,4},{8,9},{9,10},{10,1... | collective-permute-start | bytes 61448 | tf_op jit(solution)/shard_map/ppermute | solution.py:257
  31.9 3.8 %collective-permute-start.4 = (f32[40,128]{1,0:T(8,128)S(1)}, f32[40,128]{1,0:T(8,128)S(1)}, u32[]{:S(2)}, u32[]{:S(2)}) collective-permute-start(f32[40,128]{1,0:T(8,128)S(1)} %get-tuple-element.25), channel_id=1, source_target_pairs={{0,3},{1,0},{2,1},{3,2},{4,7},{5,4},{6,5},{7,6},{8,11},{9,8},{10,9... | collective-permute-start | bytes 61448 | tf_op jit(solution)/shard_map/ppermute | solution.py:257
  36.5 12.7 %all-to-all-start.1 = ((f32[8,40,128]{2,1,0:T(8,128)}), f32[8,40,128]{2,1,0:T(8,128)S(1)}, u32[]{:S(2)}, u32[]{:S(2)}) async-start(f32[8,40,128]{2,1,0:T(8,128)} %broadcast_in_dim.9), calls=%async_computation.1 | async-start | bytes 327680 | tf_op jit(solution)/shard_map/all_to_all | solution.py:265
  39.9 9.4 %copy-start = (bf16[2,64,2048]{2,1,0:T(8,128)(2,1)S(1)}, bf16[2,64,2048]{2,1,0:T(8,128)(2,1)}, u32[]{:S(2)}) copy-start(bf16[2,64,2048]{2,1,0:T(8,128)(2,1)} %refs_2_.5) | copy-start | bytes 1572868
  39.9 6.4 %collective-permute-start.5 = (bf16[64,2048]{1,0:T(8,128)(2,1)S(1)}, bf16[64,2048]{1,0:T(8,128)(2,1)S(1)}, u32[]{:S(2)}, u32[]{:S(2)}) collective-permute-start(bf16[64,2048]{1,0:T(8,128)(2,1)S(1)} %slice_bitcast_fusion.1), channel_id=1, source_target_pairs={{0,1},{1,2},{2,3},{3,0},{4,5},{5,6},{6,7},{7,4},{8,9},{9,10},{10,1... | collective-permute-start | bytes 786440 | tf_op jit(solution)/shard_map/ppermute | solution.py:259
  40.7 7.3 %collective-permute-start.6 = (bf16[64,2048]{1,0:T(8,128)(2,1)S(1)}, bf16[64,2048]{1,0:T(8,128)(2,1)S(1)}, u32[]{:S(2)}, u32[]{:S(2)}) collective-permute-start(bf16[64,2048]{1,0:T(8,128)(2,1)S(1)} %slice_bitcast_fusion), channel_id=1, source_target_pairs={{0,3},{1,0},{2,1},{3,2},{4,7},{5,4},{6,5},{7,6},{8,11},{9,8},{10,9... | collective-permute-start | bytes 786440 | tf_op jit(solution)/shard_map/ppermute | solution.py:259
  51.6 19.5 %collective-permute-start.7 = (bf16[2,256,128]{2,1,0:T(8,128)(2,1)S(1)}, bf16[2,256,128]{2,1,0:T(8,128)(2,1)S(1)}, u32[]{:S(2)}, u32[]{:S(2)}) collective-permute-start(bf16[2,256,128]{2,1,0:T(8,128)(2,1)S(1)} %get-tuple-element.34), channel_id=1, source_target_pairs={{0,16},{4,20},{8,24},{12,28},{16,0},{20,4},{24,8},{28,12},{1,17},{... | collective-permute-start | bytes 393224 | tf_op jit(solution)/shard_map/ppermute | solution.py:292
  56.3 17.7 %collective-permute-start.8 = (bf16[2,256,128]{2,1,0:T(8,128)(2,1)S(1)}, bf16[2,256,128]{2,1,0:T(8,128)(2,1)S(1)}, u32[]{:S(2)}, u32[]{:S(2)}) collective-permute-start(bf16[2,256,128]{2,1,0:T(8,128)(2,1)S(1)} %get-tuple-element.35), channel_id=1, source_target_pairs={{0,20},{4,24},{8,28},{12,0},{16,4},{20,8},{24,12},{28,16},{1,21},{... | collective-permute-start | bytes 393224 | tf_op jit(solution)/shard_map/ppermute | solution.py:292
  59.3 14.8 %collective-permute-start.9 = (bf16[2,256,128]{2,1,0:T(8,128)(2,1)S(1)}, bf16[2,256,128]{2,1,0:T(8,128)(2,1)S(1)}, u32[]{:S(2)}, u32[]{:S(2)}) collective-permute-start(bf16[2,256,128]{2,1,0:T(8,128)(2,1)S(1)} %get-tuple-element.38), channel_id=1, source_target_pairs={{0,12},{4,16},{8,20},{12,24},{16,28},{20,0},{24,4},{28,8},{1,13},{... | collective-permute-start | bytes 393224 | tf_op jit(solution)/shard_map/ppermute | solution.py:292
  62.6 11.5 %collective-permute-start.10 = (bf16[2,256,128]{2,1,0:T(8,128)(2,1)S(1)}, bf16[2,256,128]{2,1,0:T(8,128)(2,1)S(1)}, u32[]{:S(2)}, u32[]{:S(2)}) collective-permute-start(bf16[2,256,128]{2,1,0:T(8,128)(2,1)S(1)} %get-tuple-element.39), channel_id=1, source_target_pairs={{0,24},{4,28},{8,0},{12,4},{16,8},{20,12},{24,16},{28,20},{1,25},{... | collective-permute-start | bytes 393224 | tf_op jit(solution)/shard_map/ppermute | solution.py:292
  66.8 9.9 %collective-permute-start.11 = (bf16[2,256,128]{2,1,0:T(8,128)(2,1)S(1)}, bf16[2,256,128]{2,1,0:T(8,128)(2,1)S(1)}, u32[]{:S(2)}, u32[]{:S(2)}) collective-permute-start(bf16[2,256,128]{2,1,0:T(8,128)(2,1)S(1)} %get-tuple-element.40), channel_id=1, source_target_pairs={{0,8},{4,12},{8,16},{12,20},{16,24},{20,28},{24,0},{28,4},{1,9},{5... | collective-permute-start | bytes 393224 | tf_op jit(solution)/shard_map/ppermute | solution.py:292
  70.4 0.7 copy-start.3
  71.1 9.2 %copy-start.5 = (bf16[2,256,128]{2,1,0:T(8,128)(2,1)}, bf16[2,256,128]{2,1,0:T(8,128)(2,1)S(1)}, u32[]{:S(2)}) copy-start(bf16[2,256,128]{2,1,0:T(8,128)(2,1)S(1)} %collective-permute-done.7.refs_0_) | copy-start | bytes 393220
  71.1 5.6 %collective-permute-start.12 = (bf16[2,256,128]{2,1,0:T(8,128)(2,1)S(1)}, bf16[2,256,128]{2,1,0:T(8,128)(2,1)S(1)}, u32[]{:S(2)}, u32[]{:S(2)}) collective-permute-start(bf16[2,256,128]{2,1,0:T(8,128)(2,1)S(1)} %get-tuple-element.41), channel_id=1, source_target_pairs={{0,28},{4,0},{8,4},{12,8},{16,12},{20,16},{24,20},{28,24},{1,29},{... | collective-permute-start | bytes 393224 | tf_op jit(solution)/shard_map/ppermute | solution.py:292
  74.0 6.2 %copy-start.6 = (bf16[2,256,128]{2,1,0:T(8,128)(2,1)}, bf16[2,256,128]{2,1,0:T(8,128)(2,1)S(1)}, u32[]{:S(2)}) copy-start(bf16[2,256,128]{2,1,0:T(8,128)(2,1)S(1)} %collective-permute-done.8.refs_1_) | copy-start | bytes 393220
  74.0 6.2 %collective-permute-start.13 = (bf16[2,256,128]{2,1,0:T(8,128)(2,1)S(1)}, bf16[2,256,128]{2,1,0:T(8,128)(2,1)S(1)}, u32[]{:S(2)}, u32[]{:S(2)}) collective-permute-start(bf16[2,256,128]{2,1,0:T(8,128)(2,1)S(1)} %get-tuple-element.42), channel_id=1, source_target_pairs={{0,4},{4,8},{8,12},{12,16},{16,20},{20,24},{24,28},{28,0},{1,5},{5... | collective-permute-start | bytes 393224 | tf_op jit(solution)/shard_map/ppermute | solution.py:292
  74.1 6.2 %copy-start.7 = (bf16[2,256,128]{2,1,0:T(8,128)(2,1)}, bf16[2,256,128]{2,1,0:T(8,128)(2,1)S(1)}, u32[]{:S(2)}) copy-start(bf16[2,256,128]{2,1,0:T(8,128)(2,1)S(1)} %collective-permute-done.9.refs_2_) | copy-start | bytes 393220
  74.1 6.2 %copy-start.8 = (bf16[2,256,128]{2,1,0:T(8,128)(2,1)}, bf16[2,256,128]{2,1,0:T(8,128)(2,1)S(1)}, u32[]{:S(2)}) copy-start(bf16[2,256,128]{2,1,0:T(8,128)(2,1)S(1)} %collective-permute-done.10.refs_3_) | copy-start | bytes 393220
  76.6 3.6 %copy-start.9 = (bf16[2,256,128]{2,1,0:T(8,128)(2,1)}, bf16[2,256,128]{2,1,0:T(8,128)(2,1)S(1)}, u32[]{:S(2)}) copy-start(bf16[2,256,128]{2,1,0:T(8,128)(2,1)S(1)} %collective-permute-done.11.refs_4_) | copy-start | bytes 393220
  76.7 3.6 %copy-start.10 = (bf16[2,256,128]{2,1,0:T(8,128)(2,1)}, bf16[2,256,128]{2,1,0:T(8,128)(2,1)S(1)}, u32[]{:S(2)}) copy-start(bf16[2,256,128]{2,1,0:T(8,128)(2,1)S(1)} %collective-permute-done.12.refs_5_) | copy-start | bytes 393220
  80.2 0.7 copy-start.11

commit v3 on v2

--- a/solution.py
+++ b/solution.py
@@ -118,8 +118,7 @@
     out[blocks + 1 :, :] = jnp.zeros((out.shape[0] - blocks - 1, LANES), jnp.float32)
 
 
-def vectors_kernel(offsets, place, rho_ref, parts, values, flags, *refs):
-    first = len(refs) == 14
+def vectors_kernel(offsets, first, place, rho_ref, parts, values, flags, *refs):
     if first:
         zrow, own, left, right, far0, far1, *outs, zhat, far = refs[:-4]
     else:
@@ -194,19 +193,6 @@
                 outs[k][c, pl.ds(pl.multiple_of(source * share, share), share), :] = jnp.where(dead, plain, got).astype(
                     jnp.bfloat16
                 )
-
-
-def assemble_kernel(order, place, *refs):
-    pieces, out, sems = refs[:-2], refs[-2], refs[-1]
-    nz = len(pieces)
-    copies = []
-    for k, (offset, piece) in enumerate(zip(order, pieces)):
-        source = lax.rem(place[1] + nz - offset, nz)
-        copy = pltpu.make_async_copy(piece, out.at[:, source], sems.at[k])
-        copy.start()
-        copies.append(copy)
-    for copy in copies:
-        copy.wait()
 
 
 def local(child_vectors, child_values, deflated, order, coupling):
@@ -263,42 +249,42 @@
     lines = lax.broadcasted_iota(jnp.int32, block.shape, 0)
     parts = jnp.broadcast_to(jnp.where(lines < blocks, product, block), (nz,) + block.shape)
     parts = lax.all_to_all(parts, "z", 0, 0, tiled=True)
-    order = (4, 5, 3, 6, 2, 7, 1, 0)
+    calls = ((4,), (5, 3), (6, 2), (7, 1), (0,))
+    order = sum(calls, ())
     piece = jax.ShapeDtypeStruct((2, nx * rows, LANES), jnp.bfloat16)
     wide = jax.ShapeDtypeStruct((8, full), jnp.float32)
     held = (zrow,)
     pieces = []
-    for at in range(0, nz, 2):
-        pair = order[at : at + 2]
+    for at, some in enumerate(calls):
+        wait = {3: 0, 4: 1}.get(at)
+        if wait is not None:
+            pieces[wait], *held = lax.optimization_barrier((pieces[wait], *held))
         extra = (wide, wide) if at == 0 else ()
         *made, = pl.pallas_call(
-            functools.partial(vectors_kernel, pair),
-            out_shape=(piece,) * 2 + extra,
+            functools.partial(vectors_kernel, some, at == 0),
+            out_shape=(piece,) * len(some) + extra,
             in_specs=[scalar(), scalar()] + [whole()] * (8 + len(held)),
-            out_specs=(whole(),) * (2 + len(extra)),
+            out_specs=(whole(),) * (len(some) + len(extra)),
             scratch_shapes=[
-                pltpu.VMEM((2 * LANES, full), jnp.bfloat16),
+                pltpu.VMEM((len(some) * LANES, full), jnp.bfloat16),
                 pltpu.VMEM((64, full), jnp.float32),
-                pltpu.VMEM((2 * LANES, LANES), jnp.float32),
-                pltpu.VMEM((2 * LANES, LANES), jnp.float32),
+                pltpu.VMEM((len(some) * LANES, LANES), jnp.float32),
+                pltpu.VMEM((len(some) * LANES, LANES), jnp.float32),
             ],
             compiler_params=pltpu.CompilerParams(vmem_limit_bytes=24 * 1024 * 1024),
             name="vectors",
         )(place, coupling, parts, values, flags, *held, child_vectors, left, right, *opposite)
         if at == 0:
-            held = tuple(made[2:])
-        for offset, block in zip(pair, made[:2]):
+            held = tuple(made[len(some) :])
+        for offset, block in zip(some, made):
             if offset:
                 block = lax.ppermute(block, "z", [(i, (i + offset) % nz) for i in range(nz)])
             pieces.append(block)
-    eigenvectors = pl.pallas_call(
-        functools.partial(assemble_kernel, order),
-        out_shape=jax.ShapeDtypeStruct((2, nz, nx * rows, LANES), jnp.bfloat16),
-        in_specs=[scalar()] + [whole()] * nz,
-        out_specs=pl.BlockSpec(memory_space=pl.ANY),
-        scratch_shapes=[pltpu.SemaphoreType.DMA((nz,))],
-        name="assemble",
-    )(place, *pieces).reshape(full, LANES)
+    eigenvectors = jnp.zeros((2, nz, nx * rows, LANES), jnp.bfloat16)
+    for offset, block in zip(order, pieces):
+        source = lax.rem(z + nz - offset, nz)
+        eigenvectors = lax.dynamic_update_slice(eigenvectors, block[:, None], (0, source, 0, 0))
+    eigenvectors = eigenvectors.reshape(full, LANES)
     return eig.reshape(LANES), eigenvectors
 
 

time: 84.3 us -> 84.5 us (level)
  starting transfers between devices: 38.2 us -> 40.2 us
  Pallas kernels: 15.5 us -> 14.5 us
    ppermute x1, waiting for transfers between devices: 4.25 us -> 0.09 us  [local(): lax.ppermute(left[0], 'x', ahead)]
    ppermute x1, waiting for transfers between devices: 1.66 us -> 5.82 us  [local(): lax.ppermute(right[1], 'x', back)]
    ppermute x7, starting transfers between devices: 14.6 us -> 16.7 us  [local(): lax.ppermute(block, 'z', [(i, (i + offset) % nz) for i in range(nz)])]
    ppermute x7, waiting for transfers between devices: 6.14 us -> 4.65 us  [local(): lax.ppermute(block, 'z', [(i, (i + offset) % nz) for i in range(nz)])]
    pallas_call x5, Pallas kernels: 11.8 us -> 10.8 us  [local(): pl.pallas_call(functools.partial(vectors_kernel, some, at == 0), out_shap...]
  transfers between devices with their start and end apart: 16 -> 16, of which waited for: 9 -> 11; matrix products, arithmetic and copies ran while one was open for 2% -> 3% of each run, Pallas kernels for 9% -> 11%
where the time goes in v3:
time: 84.5 us; the launch traced here: 83.7 us
  starting transfers between devices  40.2 us (48%)
  waiting for transfers between devices  23.7 us (28%)
  Pallas kernels  14.5 us (17%)
  local copies, waits for them, and re-layouts  2.82 us (3%)
  between operations  1.44 us (2%)
  other arithmetic  0.99 us (1%)
    ppermute x7, starting transfers between devices, local(): lax.ppermute(block, 'z', [(i, (i + offset) % nz) for i in range(nz)])  16.7 us
    all_to_all x1, starting transfers between devices, local(): edges = lax.all_to_all(edge, ('z', 'x'), 0, 0, tiled=True)  11.7 us
    pallas_call x5, Pallas kernels, local(): pl.pallas_call(functools.partial(vectors_kernel, some, at == 0), out_shap...  10.8 us
    all_to_all x1, waiting for transfers between devices, local(): edges = lax.all_to_all(edge, ('z', 'x'), 0, 0, tiled=True)  8.13 us
    ppermute x1, waiting for transfers between devices, local(): lax.ppermute(right[1], 'x', back)  5.82 us
    ppermute x7, waiting for transfers between devices, local(): lax.ppermute(block, 'z', [(i, (i + offset) % nz) for i in range(nz)])  4.65 us
    ppermute x3, starting transfers between devices, local(): lax.ppermute(block, 'x', [(i, (i + k) % nx) for i in range(nx)])  4.15 us
    pallas_call x1, Pallas kernels, local(): pl.pallas_call(roots_kernel, out_shape=(jax.ShapeDtypeStruct((blocks + 8,...  3.68 us
  transfers between devices with their start and end apart: 16, of which 11 were waited for; matrix products, arithmetic and copies ran while one was open for 3% of the time, Pallas kernels for 11%

profile of v3, /device:TPU:26, one launch (start us, length us, event | category | flops | bytes accessed | tf_op | source)
XLA Modules:
  0.0 83.7 jit_solution(10776289968778228072)
XLA Ops:
  0.6 1.6 %collective-permute-start = (bf16[2,64,2048]{2,1,0:T(8,128)(2,1)}, bf16[2,64,2048]{2,1,0:T(8,128)(2,1)S(1)}, u32[]{:S(2)}, u32[]{:S(2)}) collective-permute-start(bf16[2,64,2048]{2,1,0:T(8,128)(2,1)} %refs_2_.7), channel_id=1, source_target_pairs={{0,1},{1,2},{2,3},{3,0},{4,5},{5,6},{6,7},{7,4},{8,9},{9,10},{10,1... | collective-permute-start | bytes 1572872 | tf_op jit(solution)/shard_map/ppermute | solution.py:213
  2.7 0.8 fusion
  3.6 0.7 broadcast_in_dim.35
  4.2 11.7 %all-to-all-start = ((bf16[32,16,128]{2,1,0:T(8,128)(2,1)}), bf16[32,16,128]{2,1,0:T(8,128)(2,1)S(1)}, u32[]{:S(2)}, u32[]{:S(2)}) async-start(bf16[32,16,128]{2,1,0:T(8,128)(2,1)} %broadcast_in_dim.35), calls=%async_computation | async-start | bytes 262144 | tf_op jit(solution)/shard_map/all_to_all | solution.py:219
  16.7 8.1 %all-to-all-done.edges = bf16[32,16,128]{2,1,0:T(8,128)(2,1)S(1)} async-done(((bf16[32,16,128]{2,1,0:T(8,128)(2,1)}), bf16[32,16,128]{2,1,0:T(8,128)(2,1)S(1)}, u32[]{:S(2)}, u32[]{:S(2)}) %all-to-all-start) | async-done | bytes 131104 | tf_op jit(solution)/shard_map/all_to_all | solution.py:219
  24.9 3.7 %roots.1 = (f32[40,128]{1,0:T(8,128)S(1)}, f32[1,128]{1,0:T(1,128)}, f32[1,4096]{1,0:T(1,128)S(1)}) custom-call(s32[3]{0:T(128)S(1)} %pad_add_fusion.place, f32[1]{0:T(128)S(6)} %copy.16.rho_ref, bf16[32,16,128]{2,1,0:T(8,128)(2,1)S(1)} %all-to-all-done.edges, f32[1,4096]{1,0:T(1,128)S(1)} %bitcast.30, s32[1,4096]{1,0:T(1,128)S(1)} %bitcast.36), custom_call_target="tpu_custom_call" | custom-call | tf_op jit(solution)/shard_map/roots/pallas_call | solution.py:223
  28.5 2.1 %collective-permute-start.2 = (f32[40,128]{1,0:T(8,128)S(1)}, f32[40,128]{1,0:T(8,128)S(1)}, u32[]{:S(2)}, u32[]{:S(2)}) collective-permute-start(f32[40,128]{1,0:T(8,128)S(1)} %get-tuple-element.30), channel_id=1, source_target_pairs={{0,2},{1,3},{2,0},{3,1},{4,6},{5,7},{6,4},{7,5},{8,10},{9,11},{10,... | collective-permute-start | bytes 61448 | tf_op jit(solution)/shard_map/ppermute | solution.py:243
  30.7 1.3 %collective-permute-start.3 = (f32[40,128]{1,0:T(8,128)S(1)}, f32[40,128]{1,0:T(8,128)S(1)}, u32[]{:S(2)}, u32[]{:S(2)}) collective-permute-start(f32[40,128]{1,0:T(8,128)S(1)} %get-tuple-element.30), channel_id=1, source_target_pairs={{0,1},{1,2},{2,3},{3,0},{4,5},{5,6},{6,7},{7,4},{8,9},{9,10},{10,1... | collective-permute-start | bytes 61448 | tf_op jit(solution)/shard_map/ppermute | solution.py:243
  31.9 0.8 collective-permute-start.4
  32.7 1.1 %collective-permute-done.2 = f32[40,128]{1,0:T(8,128)S(1)} collective-permute-done((f32[40,128]{1,0:T(8,128)S(1)}, f32[40,128]{1,0:T(8,128)S(1)}, u32[]{:S(2)}, u32[]{:S(2)}) %collective-permute-start.2) | collective-permute-done | bytes 20512 | tf_op jit(solution)/shard_map/ppermute | solution.py:243
  33.8 0.6 collective-permute-done.3
  34.5 1.3 %collective-permute-done.4 = f32[40,128]{1,0:T(8,128)S(1)} collective-permute-done((f32[40,128]{1,0:T(8,128)S(1)}, f32[40,128]{1,0:T(8,128)S(1)}, u32[]{:S(2)}, u32[]{:S(2)}) %collective-permute-start.4) | collective-permute-done | bytes 20512 | tf_op jit(solution)/shard_map/ppermute | solution.py:243
  35.7 0.8 collective-permute-start.5
  36.6 0.7 broadcast_in_dim.37
  37.3 3.4 %all-to-all-start.1 = ((f32[8,40,128]{2,1,0:T(8,128)}), f32[8,40,128]{2,1,0:T(8,128)S(1)}, u32[]{:S(2)}, u32[]{:S(2)}) async-start(f32[8,40,128]{2,1,0:T(8,128)} %broadcast_in_dim.37), calls=%async_computation.1 | async-start | bytes 327680 | tf_op jit(solution)/shard_map/all_to_all | solution.py:251
  40.7 1.4 %collective-permute-start.6 = (bf16[64,2048]{1,0:T(8,128)(2,1)S(1)}, bf16[64,2048]{1,0:T(8,128)(2,1)S(1)}, u32[]{:S(2)}, u32[]{:S(2)}) collective-permute-start(bf16[64,2048]{1,0:T(8,128)(2,1)S(1)} %slice_bitcast_fusion), channel_id=1, source_target_pairs={{0,3},{1,0},{2,1},{3,2},{4,7},{5,4},{6,5},{7,6},{8,11},{9,8},{10,9... | collective-permute-start | bytes 786440 | tf_op jit(solution)/shard_map/ppermute | solution.py:245
  42.2 5.8 %collective-permute-done.6.refs_5_.refs_6_ = bf16[64,2048]{1,0:T(8,128)(2,1)S(1)} collective-permute-done((bf16[64,2048]{1,0:T(8,128)(2,1)S(1)}, bf16[64,2048]{1,0:T(8,128)(2,1)S(1)}, u32[]{:S(2)}, u32[]{:S(2)}) %collective-permute-start.6) | collective-permute-done | bytes 262176 | tf_op jit(solution)/shard_map/ppermute | solution.py:245
  48.0 2.0 %all-to-all-done.1.parts = f32[8,40,128]{2,1,0:T(8,128)S(1)} async-done(((f32[8,40,128]{2,1,0:T(8,128)}), f32[8,40,128]{2,1,0:T(8,128)S(1)}, u32[]{:S(2)}, u32[]{:S(2)}) %all-to-all-start.1) | async-done | bytes 163872 | tf_op jit(solution)/shard_map/all_to_all | solution.py:251
  50.0 1.8 %vectors.5 = (bf16[2,256,128]{2,1,0:T(8,128)(2,1)S(1)}, f32[8,4096]{1,0:T(8,128)S(1)}, f32[8,4096]{1,0:T(8,128)S(1)}) custom-call(s32[3]{0:T(128)S(1)} %pad_add_fusion.place, f32[1]{0:T(128)S(6)} %copy.16.rho_ref, f32[8,40,128]{2,1,0:T(8,128)S(1)} %all-to-all-done.1.parts, f32[1,4096]{1,0:T(1,128)S(1)} %bitcast.31, s32[1,4096]{1,0:T(1,128)S(1)} %bitcast.37, ...), custom_call_target="tpu_custom_call" | custom-call | tf_op jit(solution)/shard_map/vectors/pallas_call | solution.py:263
  51.9 4.1 %collective-permute-start.7 = (bf16[2,256,128]{2,1,0:T(8,128)(2,1)S(1)}, bf16[2,256,128]{2,1,0:T(8,128)(2,1)S(1)}, u32[]{:S(2)}, u32[]{:S(2)}) collective-permute-start(bf16[2,256,128]{2,1,0:T(8,128)(2,1)S(1)} %get-tuple-element.39), channel_id=1, source_target_pairs={{0,16},{4,20},{8,24},{12,28},{16,0},{20,4},{24,8},{28,12},{1,17},{... | collective-permute-start | bytes 393224 | tf_op jit(solution)/shard_map/ppermute | solution.py:281
  56.0 2.4 %vectors.6 = (bf16[2,256,128]{2,1,0:T(8,128)(2,1)S(1)}, bf16[2,256,128]{2,1,0:T(8,128)(2,1)S(1)}) custom-call(s32[3]{0:T(128)S(1)} %pad_add_fusion.place, f32[1]{0:T(128)S(6)} %copy.16.rho_ref, f32[8,40,128]{2,1,0:T(8,128)S(1)} %all-to-all-done.1.parts, f32[1,4096]{1,0:T(1,128)S(1)} %bitcast.32, s32[1,4096]{1,0:T(1,128)S(1)} %bitcast.38, ...), custom_call_target="tpu_custom_call" | custom-call | tf_op jit(solution)/shard_map/vectors/pallas_call | solution.py:263
  58.3 1.3 %collective-permute-start.8 = (bf16[2,256,128]{2,1,0:T(8,128)(2,1)S(1)}, bf16[2,256,128]{2,1,0:T(8,128)(2,1)S(1)}, u32[]{:S(2)}, u32[]{:S(2)}) collective-permute-start(bf16[2,256,128]{2,1,0:T(8,128)(2,1)S(1)} %get-tuple-element.43), channel_id=1, source_target_pairs={{0,20},{4,24},{8,28},{12,0},{16,4},{20,8},{24,12},{28,16},{1,21},{... | collective-permute-start | bytes 393224 | tf_op jit(solution)/shard_map/ppermute | solution.py:281
  59.6 2.4 %vectors.7 = (bf16[2,256,128]{2,1,0:T(8,128)(2,1)S(1)}, bf16[2,256,128]{2,1,0:T(8,128)(2,1)S(1)}) custom-call(s32[3]{0:T(128)S(1)} %pad_add_fusion.place, f32[1]{0:T(128)S(6)} %copy.16.rho_ref, f32[8,40,128]{2,1,0:T(8,128)S(1)} %all-to-all-done.1.parts, f32[1,4096]{1,0:T(1,128)S(1)} %bitcast.33, s32[1,4096]{1,0:T(1,128)S(1)} %bitcast.39, ...), custom_call_target="tpu_custom_call" | custom-call | tf_op jit(solution)/shard_map/vectors/pallas_call | solution.py:263
  62.0 2.1 %collective-permute-start.10 = (bf16[2,256,128]{2,1,0:T(8,128)(2,1)S(1)}, bf16[2,256,128]{2,1,0:T(8,128)(2,1)S(1)}, u32[]{:S(2)}, u32[]{:S(2)}) collective-permute-start(bf16[2,256,128]{2,1,0:T(8,128)(2,1)S(1)} %get-tuple-element.48), channel_id=1, source_target_pairs={{0,24},{4,28},{8,0},{12,4},{16,8},{20,12},{24,16},{28,20},{1,25},{... | collective-permute-start | bytes 393224 | tf_op jit(solution)/shard_map/ppermute | solution.py:281
  64.1 1.1 %collective-permute-start.9 = (bf16[2,256,128]{2,1,0:T(8,128)(2,1)S(1)}, bf16[2,256,128]{2,1,0:T(8,128)(2,1)S(1)}, u32[]{:S(2)}, u32[]{:S(2)}) collective-permute-start(bf16[2,256,128]{2,1,0:T(8,128)(2,1)S(1)} %get-tuple-element.47), channel_id=1, source_target_pairs={{0,12},{4,16},{8,20},{12,24},{16,28},{20,0},{24,4},{28,8},{1,13},{... | collective-permute-start | bytes 393224 | tf_op jit(solution)/shard_map/ppermute | solution.py:281
  65.2 3.6 %collective-permute-start.11 = (bf16[2,256,128]{2,1,0:T(8,128)(2,1)S(1)}, bf16[2,256,128]{2,1,0:T(8,128)(2,1)S(1)}, u32[]{:S(2)}, u32[]{:S(2)}) collective-permute-start(bf16[2,256,128]{2,1,0:T(8,128)(2,1)S(1)} %get-tuple-element.49), channel_id=1, source_target_pairs={{0,8},{4,12},{8,16},{12,20},{16,24},{20,28},{24,0},{28,4},{1,9},{5... | collective-permute-start | bytes 393224 | tf_op jit(solution)/shard_map/ppermute | solution.py:281
  68.8 0.7 collective-permute-done.8
  69.5 2.4 %vectors.8 = (bf16[2,256,128]{2,1,0:T(8,128)(2,1)S(1)}, bf16[2,256,128]{2,1,0:T(8,128)(2,1)S(1)}) custom-call(s32[3]{0:T(128)S(1)} %pad_add_fusion.place, f32[1]{0:T(128)S(6)} %copy.16.rho_ref, f32[8,40,128]{2,1,0:T(8,128)S(1)} %all-to-all-done.1.parts, f32[1,4096]{1,0:T(1,128)S(1)} %bitcast.34, s32[1,4096]{1,0:T(1,128)S(1)} %bitcast.40, ...), custom_call_target="tpu_custom_call" | custom-call | tf_op jit(solution)/shard_map/vectors/pallas_call | solution.py:263
  71.9 4.5 %collective-permute-start.12 = (bf16[2,256,128]{2,1,0:T(8,128)(2,1)S(1)}, bf16[2,256,128]{2,1,0:T(8,128)(2,1)S(1)}, u32[]{:S(2)}, u32[]{:S(2)}) collective-permute-start(bf16[2,256,128]{2,1,0:T(8,128)(2,1)S(1)} %get-tuple-element.50), channel_id=1, source_target_pairs={{0,28},{4,0},{8,4},{12,8},{16,12},{20,16},{24,20},{28,24},{1,29},{... | collective-permute-start | bytes 393224 | tf_op jit(solution)/shard_map/ppermute | solution.py:281
  76.6 1.8 %vectors.9 = bf16[2,256,128]{2,1,0:T(8,128)(2,1)S(1)} custom-call(s32[3]{0:T(128)S(1)} %pad_add_fusion.place, f32[1]{0:T(128)S(6)} %copy.16.rho_ref, f32[8,40,128]{2,1,0:T(8,128)S(1)} %all-to-all-done.1.parts, f32[1,4096]{1,0:T(1,128)S(1)} %bitcast.35, s32[1,4096]{1,0:T(1,128)S(1)} %bitcast.41, f32[8,4096]{1,0:T(8,128)S(1)} %get-tuple-element.52.refs_0_, ...), custom_call_target="tpu_custom_call" | custom-call | tf_op jit(solution)/shard_map/vectors/pallas_call | solution.py:263
  79.1 3.5 %collective-permute-done.13 = bf16[2,256,128]{2,1,0:T(8,128)(2,1)S(1)} collective-permute-done((bf16[2,256,128]{2,1,0:T(8,128)(2,1)S(1)}, bf16[2,256,128]{2,1,0:T(8,128)(2,1)S(1)}, u32[]{:S(2)}, u32[]{:S(2)}) %collective-permute-start.13) | collective-permute-done | bytes 131104 | tf_op jit(solution)/shard_map/ppermute | solution.py:281
  82.7 1.0 %copy-done.3 = bf16[2,8,256,128]{3,2,1,0:T(8,128)(2,1)} copy-done((bf16[2,8,256,128]{3,2,1,0:T(8,128)(2,1)}, bf16[2,8,256,128]{3,2,1,0:T(8,128)(2,1)S(1)}, u32[]{:S(2)}) %copy-start.3) | copy-done | bytes 1048600
  (32 shorter events, 1.8 us)
Async XLA Ops:
  0.6 16.1 %collective-permute-start = (bf16[2,64,2048]{2,1,0:T(8,128)(2,1)}, bf16[2,64,2048]{2,1,0:T(8,128)(2,1)S(1)}, u32[]{:S(2)}, u32[]{:S(2)}) collective-permute-start(bf16[2,64,2048]{2,1,0:T(8,128)(2,1)} %refs_2_.7), channel_id=1, source_target_pairs={{0,1},{1,2},{2,3},{3,0},{4,5},{5,6},{6,7},{7,4},{8,9},{9,10},{10,1... | collective-permute-start | bytes 1572872 | tf_op jit(solution)/shard_map/ppermute | solution.py:213
  2.2 14.5 %collective-permute-start.1 = (bf16[2,64,2048]{2,1,0:T(8,128)(2,1)}, bf16[2,64,2048]{2,1,0:T(8,128)(2,1)S(1)}, u32[]{:S(2)}, u32[]{:S(2)}) collective-permute-start(bf16[2,64,2048]{2,1,0:T(8,128)(2,1)} %refs_2_.7), channel_id=1, source_target_pairs={{0,3},{1,0},{2,1},{3,2},{4,7},{5,4},{6,5},{7,6},{8,11},{9,8},{10,9... | collective-permute-start | bytes 1572872 | tf_op jit(solution)/shard_map/ppermute | solution.py:214
  4.2 20.6 %copy-start.1 = (f32[4096]{0:T(1024)S(1)}, f32[4096]{0:T(1024)}, u32[]{:S(2)}) copy-start(f32[4096]{0:T(1024)} %param.6) | copy-start | bytes 49156
  4.2 20.6 %copy-start.2 = (s32[4096]{0:T(1024)S(1)}, s32[4096]{0:T(1024)}, u32[]{:S(2)}) copy-start(s32[4096]{0:T(1024)} %param.7) | copy-start | bytes 49156
  4.2 20.6 %all-to-all-start = ((bf16[32,16,128]{2,1,0:T(8,128)(2,1)}), bf16[32,16,128]{2,1,0:T(8,128)(2,1)S(1)}, u32[]{:S(2)}, u32[]{:S(2)}) async-start(bf16[32,16,128]{2,1,0:T(8,128)(2,1)} %broadcast_in_dim.35), calls=%async_computation | async-start | bytes 262144 | tf_op jit(solution)/shard_map/all_to_all | solution.py:219
  28.5 5.3 %collective-permute-start.2 = (f32[40,128]{1,0:T(8,128)S(1)}, f32[40,128]{1,0:T(8,128)S(1)}, u32[]{:S(2)}, u32[]{:S(2)}) collective-permute-start(f32[40,128]{1,0:T(8,128)S(1)} %get-tuple-element.30), channel_id=1, source_target_pairs={{0,2},{1,3},{2,0},{3,1},{4,6},{5,7},{6,4},{7,5},{8,10},{9,11},{10,... | collective-permute-start | bytes 61448 | tf_op jit(solution)/shard_map/ppermute | solution.py:243
  30.7 3.8 %collective-permute-start.3 = (f32[40,128]{1,0:T(8,128)S(1)}, f32[40,128]{1,0:T(8,128)S(1)}, u32[]{:S(2)}, u32[]{:S(2)}) collective-permute-start(f32[40,128]{1,0:T(8,128)S(1)} %get-tuple-element.30), channel_id=1, source_target_pairs={{0,1},{1,2},{2,3},{3,0},{4,5},{5,6},{6,7},{7,4},{8,9},{9,10},{10,1... | collective-permute-start | bytes 61448 | tf_op jit(solution)/shard_map/ppermute | solution.py:243
  31.9 3.8 %collective-permute-start.4 = (f32[40,128]{1,0:T(8,128)S(1)}, f32[40,128]{1,0:T(8,128)S(1)}, u32[]{:S(2)}, u32[]{:S(2)}) collective-permute-start(f32[40,128]{1,0:T(8,128)S(1)} %get-tuple-element.30), channel_id=1, source_target_pairs={{0,3},{1,0},{2,1},{3,2},{4,7},{5,4},{6,5},{7,6},{8,11},{9,8},{10,9... | collective-permute-start | bytes 61448 | tf_op jit(solution)/shard_map/ppermute | solution.py:243
  35.7 6.4 %collective-permute-start.5 = (bf16[64,2048]{1,0:T(8,128)(2,1)S(1)}, bf16[64,2048]{1,0:T(8,128)(2,1)S(1)}, u32[]{:S(2)}, u32[]{:S(2)}) collective-permute-start(bf16[64,2048]{1,0:T(8,128)(2,1)S(1)} %slice_bitcast_fusion.1), channel_id=1, source_target_pairs={{0,1},{1,2},{2,3},{3,0},{4,5},{5,6},{6,7},{7,4},{8,9},{9,10},{10,1... | collective-permute-start | bytes 786440 | tf_op jit(solution)/shard_map/ppermute | solution.py:245
  36.6 13.4 %copy-start = (bf16[2,64,2048]{2,1,0:T(8,128)(2,1)S(1)}, bf16[2,64,2048]{2,1,0:T(8,128)(2,1)}, u32[]{:S(2)}) copy-start(bf16[2,64,2048]{2,1,0:T(8,128)(2,1)} %refs_2_.7) | copy-start | bytes 1572868
  37.3 12.7 %all-to-all-start.1 = ((f32[8,40,128]{2,1,0:T(8,128)}), f32[8,40,128]{2,1,0:T(8,128)S(1)}, u32[]{:S(2)}, u32[]{:S(2)}) async-start(f32[8,40,128]{2,1,0:T(8,128)} %broadcast_in_dim.37), calls=%async_computation.1 | async-start | bytes 327680 | tf_op jit(solution)/shard_map/all_to_all | solution.py:251
  40.7 7.3 %collective-permute-start.6 = (bf16[64,2048]{1,0:T(8,128)(2,1)S(1)}, bf16[64,2048]{1,0:T(8,128)(2,1)S(1)}, u32[]{:S(2)}, u32[]{:S(2)}) collective-permute-start(bf16[64,2048]{1,0:T(8,128)(2,1)S(1)} %slice_bitcast_fusion), channel_id=1, source_target_pairs={{0,3},{1,0},{2,1},{3,2},{4,7},{5,4},{6,5},{7,6},{8,11},{9,8},{10,9... | collective-permute-start | bytes 786440 | tf_op jit(solution)/shard_map/ppermute | solution.py:245
  51.9 17.0 %collective-permute-start.7 = (bf16[2,256,128]{2,1,0:T(8,128)(2,1)S(1)}, bf16[2,256,128]{2,1,0:T(8,128)(2,1)S(1)}, u32[]{:S(2)}, u32[]{:S(2)}) collective-permute-start(bf16[2,256,128]{2,1,0:T(8,128)(2,1)S(1)} %get-tuple-element.39), channel_id=1, source_target_pairs={{0,16},{4,20},{8,24},{12,28},{16,0},{20,4},{24,8},{28,12},{1,17},{... | collective-permute-start | bytes 393224 | tf_op jit(solution)/shard_map/ppermute | solution.py:281
  58.3 11.2 %collective-permute-start.8 = (bf16[2,256,128]{2,1,0:T(8,128)(2,1)S(1)}, bf16[2,256,128]{2,1,0:T(8,128)(2,1)S(1)}, u32[]{:S(2)}, u32[]{:S(2)}) collective-permute-start(bf16[2,256,128]{2,1,0:T(8,128)(2,1)S(1)} %get-tuple-element.43), channel_id=1, source_target_pairs={{0,20},{4,24},{8,28},{12,0},{16,4},{20,8},{24,12},{28,16},{1,21},{... | collective-permute-start | bytes 393224 | tf_op jit(solution)/shard_map/ppermute | solution.py:281
  62.0 16.5 %collective-permute-start.10 = (bf16[2,256,128]{2,1,0:T(8,128)(2,1)S(1)}, bf16[2,256,128]{2,1,0:T(8,128)(2,1)S(1)}, u32[]{:S(2)}, u32[]{:S(2)}) collective-permute-start(bf16[2,256,128]{2,1,0:T(8,128)(2,1)S(1)} %get-tuple-element.48), channel_id=1, source_target_pairs={{0,24},{4,28},{8,0},{12,4},{16,8},{20,12},{24,16},{28,20},{1,25},{... | collective-permute-start | bytes 393224 | tf_op jit(solution)/shard_map/ppermute | solution.py:281
  64.1 14.4 %collective-permute-start.9 = (bf16[2,256,128]{2,1,0:T(8,128)(2,1)S(1)}, bf16[2,256,128]{2,1,0:T(8,128)(2,1)S(1)}, u32[]{:S(2)}, u32[]{:S(2)}) collective-permute-start(bf16[2,256,128]{2,1,0:T(8,128)(2,1)S(1)} %get-tuple-element.47), channel_id=1, source_target_pairs={{0,12},{4,16},{8,20},{12,24},{16,28},{20,0},{24,4},{28,8},{1,13},{... | collective-permute-start | bytes 393224 | tf_op jit(solution)/shard_map/ppermute | solution.py:281
  65.2 13.5 %collective-permute-start.11 = (bf16[2,256,128]{2,1,0:T(8,128)(2,1)S(1)}, bf16[2,256,128]{2,1,0:T(8,128)(2,1)S(1)}, u32[]{:S(2)}, u32[]{:S(2)}) collective-permute-start(bf16[2,256,128]{2,1,0:T(8,128)(2,1)S(1)} %get-tuple-element.49), channel_id=1, source_target_pairs={{0,8},{4,12},{8,16},{12,20},{16,24},{20,28},{24,0},{28,4},{1,9},{5... | collective-permute-start | bytes 393224 | tf_op jit(solution)/shard_map/ppermute | solution.py:281
  71.9 7.2 %collective-permute-start.12 = (bf16[2,256,128]{2,1,0:T(8,128)(2,1)S(1)}, bf16[2,256,128]{2,1,0:T(8,128)(2,1)S(1)}, u32[]{:S(2)}, u32[]{:S(2)}) collective-permute-start(bf16[2,256,128]{2,1,0:T(8,128)(2,1)S(1)} %get-tuple-element.50), channel_id=1, source_target_pairs={{0,28},{4,0},{8,4},{12,8},{16,12},{20,16},{24,20},{28,24},{1,29},{... | collective-permute-start | bytes 393224 | tf_op jit(solution)/shard_map/ppermute | solution.py:281
  76.4 6.2 %collective-permute-start.13 = (bf16[2,256,128]{2,1,0:T(8,128)(2,1)S(1)}, bf16[2,256,128]{2,1,0:T(8,128)(2,1)S(1)}, u32[]{:S(2)}, u32[]{:S(2)}) collective-permute-start(bf16[2,256,128]{2,1,0:T(8,128)(2,1)S(1)} %get-tuple-element.51), channel_id=1, source_target_pairs={{0,4},{4,8},{8,12},{12,16},{16,20},{20,24},{24,28},{28,0},{1,5},{5... | collective-permute-start | bytes 393224 | tf_op jit(solution)/shard_map/ppermute | solution.py:281
  82.7 1.0 %copy-start.3 = (bf16[2,8,256,128]{3,2,1,0:T(8,128)(2,1)}, bf16[2,8,256,128]{3,2,1,0:T(8,128)(2,1)S(1)}, u32[]{:S(2)}) copy-start(bf16[2,8,256,128]{3,2,1,0:T(8,128)(2,1)S(1)} %bitcast_dynamic-update-slice_fusion) | copy-start | bytes 3145732

commit v4 on v3

--- a/solution.py
+++ b/solution.py
@@ -280,6 +280,7 @@
             if offset:
                 block = lax.ppermute(block, "z", [(i, (i + offset) % nz) for i in range(nz)])
             pieces.append(block)
+    pieces = lax.optimization_barrier(pieces[::-1])[::-1]
     eigenvectors = jnp.zeros((2, nz, nx * rows, LANES), jnp.bfloat16)
     for offset, block in zip(order, pieces):
         source = lax.rem(z + nz - offset, nz)

time: 84.5 us -> 86.2 us (1.020)
  local copies, waits for them, and re-layouts: 2.82 us -> 7.99 us
  waiting for transfers between devices: 23.7 us -> 21.5 us
  starting transfers between devices: 40.2 us -> 39 us
    ppermute x1, waiting for transfers between devices: 0.09 us -> 4.25 us  [local(): lax.ppermute(left[0], 'x', ahead)]
    ppermute x1, waiting for transfers between devices: 5.82 us -> 1.66 us  [local(): lax.ppermute(right[1], 'x', back)]
    dynamic_update_slice x9, local copies, waits for them, and re-layouts: 0.25 us -> 3.9 us  [local(): lax.dynamic_update_slice(eigenvectors, block[:, None], (0, source, 0, 0))]
    unnamed x8 -> x12, local copies, waits for them, and re-layouts: 0.98 us -> 2.5 us
    ppermute x7, waiting for transfers between devices: 4.65 us -> 3.22 us  [local(): lax.ppermute(block, 'z', [(i, (i + offset) % nz) for i in range(nz)])]
    ppermute x7, starting transfers between devices: 16.7 us -> 15.4 us  [local(): lax.ppermute(block, 'z', [(i, (i + offset) % nz) for i in range(nz)])]
  transfers between devices with their start and end apart: 16 -> 16, of which waited for: 11 -> 9; matrix products, arithmetic and copies ran while one was open for 3% -> 2% of each run, Pallas kernels for 11% -> 10%
where the time goes in v4:
time: 86.2 us; the launch traced here: 85.3 us
  starting transfers between devices  39 us (45%)
  waiting for transfers between devices  21.5 us (25%)
  Pallas kernels  14.5 us (17%)
  local copies, waits for them, and re-layouts  7.99 us (9%)
  between operations  1.46 us (2%)
  other arithmetic  0.99 us (1%)
    ppermute x7, starting transfers between devices, local(): lax.ppermute(block, 'z', [(i, (i + offset) % nz) for i in range(nz)])  15.4 us
    all_to_all x1, starting transfers between devices, local(): edges = lax.all_to_all(edge, ('z', 'x'), 0, 0, tiled=True)  11.7 us
    pallas_call x5, Pallas kernels, local(): pl.pallas_call(functools.partial(vectors_kernel, some, at == 0), out_shap...  10.8 us
    all_to_all x1, waiting for transfers between devices, local(): edges = lax.all_to_all(edge, ('z', 'x'), 0, 0, tiled=True)  8.13 us
    ppermute x1, waiting for transfers between devices, local(): lax.ppermute(left[0], 'x', ahead)  4.25 us
    ppermute x3, starting transfers between devices, local(): lax.ppermute(block, 'x', [(i, (i + k) % nx) for i in range(nx)])  4.15 us
    dynamic_update_slice x9, local copies, waits for them, and re-layouts, local(): lax.dynamic_update_slice(eigenvectors, block[:, None], (0, source, 0, 0))  3.9 us
    pallas_call x1, Pallas kernels, local(): pl.pallas_call(roots_kernel, out_shape=(jax.ShapeDtypeStruct((blocks + 8,...  3.68 us
  transfers between devices with their start and end apart: 16, of which 9 were waited for; matrix products, arithmetic and copies ran while one was open for 2% of the time, Pallas kernels for 10%

profile of v4, /device:TPU:26, one launch (start us, length us, event | category | flops | bytes accessed | tf_op | source)
XLA Modules:
  0.0 85.3 jit_solution(10970396361801523582)
XLA Ops:
  0.6 1.6 %collective-permute-start = (bf16[2,64,2048]{2,1,0:T(8,128)(2,1)}, bf16[2,64,2048]{2,1,0:T(8,128)(2,1)S(1)}, u32[]{:S(2)}, u32[]{:S(2)}) collective-permute-start(bf16[2,64,2048]{2,1,0:T(8,128)(2,1)} %refs_2_.7), channel_id=1, source_target_pairs={{0,1},{1,2},{2,3},{3,0},{4,5},{5,6},{6,7},{7,4},{8,9},{9,10},{10,1... | collective-permute-start | bytes 1572872 | tf_op jit(solution)/shard_map/ppermute | solution.py:213
  2.7 0.8 fusion
  4.2 11.7 %all-to-all-start = ((bf16[32,16,128]{2,1,0:T(8,128)(2,1)}), bf16[32,16,128]{2,1,0:T(8,128)(2,1)S(1)}, u32[]{:S(2)}, u32[]{:S(2)}) async-start(bf16[32,16,128]{2,1,0:T(8,128)(2,1)} %broadcast_in_dim.35), calls=%async_computation | async-start | bytes 262144 | tf_op jit(solution)/shard_map/all_to_all | solution.py:219
  16.7 8.1 %all-to-all-done.edges = bf16[32,16,128]{2,1,0:T(8,128)(2,1)S(1)} async-done(((bf16[32,16,128]{2,1,0:T(8,128)(2,1)}), bf16[32,16,128]{2,1,0:T(8,128)(2,1)S(1)}, u32[]{:S(2)}, u32[]{:S(2)}) %all-to-all-start) | async-done | bytes 131104 | tf_op jit(solution)/shard_map/all_to_all | solution.py:219
  24.9 3.7 %roots.1 = (f32[40,128]{1,0:T(8,128)S(1)}, f32[1,128]{1,0:T(1,128)}, f32[1,4096]{1,0:T(1,128)S(1)}) custom-call(s32[3]{0:T(128)S(1)} %pad_add_fusion.place, f32[1]{0:T(128)S(6)} %copy.19.rho_ref, bf16[32,16,128]{2,1,0:T(8,128)(2,1)S(1)} %all-to-all-done.edges, f32[1,4096]{1,0:T(1,128)S(1)} %bitcast.36, s32[1,4096]{1,0:T(1,128)S(1)} %bitcast.42), custom_call_target="tpu_custom_call" | custom-call | tf_op jit(solution)/shard_map/roots/pallas_call | solution.py:223
  28.5 2.1 %collective-permute-start.2 = (f32[40,128]{1,0:T(8,128)S(1)}, f32[40,128]{1,0:T(8,128)S(1)}, u32[]{:S(2)}, u32[]{:S(2)}) collective-permute-start(f32[40,128]{1,0:T(8,128)S(1)} %get-tuple-element.38), channel_id=1, source_target_pairs={{0,2},{1,3},{2,0},{3,1},{4,6},{5,7},{6,4},{7,5},{8,10},{9,11},{10,... | collective-permute-start | bytes 61448 | tf_op jit(solution)/shard_map/ppermute | solution.py:243
  30.7 1.3 %collective-permute-start.3 = (f32[40,128]{1,0:T(8,128)S(1)}, f32[40,128]{1,0:T(8,128)S(1)}, u32[]{:S(2)}, u32[]{:S(2)}) collective-permute-start(f32[40,128]{1,0:T(8,128)S(1)} %get-tuple-element.38), channel_id=1, source_target_pairs={{0,1},{1,2},{2,3},{3,0},{4,5},{5,6},{6,7},{7,4},{8,9},{9,10},{10,1... | collective-permute-start | bytes 61448 | tf_op jit(solution)/shard_map/ppermute | solution.py:243
  32.7 1.1 %collective-permute-done.2 = f32[40,128]{1,0:T(8,128)S(1)} collective-permute-done((f32[40,128]{1,0:T(8,128)S(1)}, f32[40,128]{1,0:T(8,128)S(1)}, u32[]{:S(2)}, u32[]{:S(2)}) %collective-permute-start.2) | collective-permute-done | bytes 20512 | tf_op jit(solution)/shard_map/ppermute | solution.py:243
  34.5 1.3 %collective-permute-done.4 = f32[40,128]{1,0:T(8,128)S(1)} collective-permute-done((f32[40,128]{1,0:T(8,128)S(1)}, f32[40,128]{1,0:T(8,128)S(1)}, u32[]{:S(2)}, u32[]{:S(2)}) %collective-permute-start.4) | collective-permute-done | bytes 20512 | tf_op jit(solution)/shard_map/ppermute | solution.py:243
  36.5 3.4 %all-to-all-start.1 = ((f32[8,40,128]{2,1,0:T(8,128)}), f32[8,40,128]{2,1,0:T(8,128)S(1)}, u32[]{:S(2)}, u32[]{:S(2)}) async-start(f32[8,40,128]{2,1,0:T(8,128)} %broadcast_in_dim.37), calls=%async_computation.1 | async-start | bytes 327680 | tf_op jit(solution)/shard_map/all_to_all | solution.py:251
  40.7 1.4 %collective-permute-start.6 = (bf16[64,2048]{1,0:T(8,128)(2,1)S(1)}, bf16[64,2048]{1,0:T(8,128)(2,1)S(1)}, u32[]{:S(2)}, u32[]{:S(2)}) collective-permute-start(bf16[64,2048]{1,0:T(8,128)(2,1)S(1)} %slice_bitcast_fusion), channel_id=1, source_target_pairs={{0,3},{1,0},{2,1},{3,2},{4,7},{5,4},{6,5},{7,6},{8,11},{9,8},{10,9... | collective-permute-start | bytes 786440 | tf_op jit(solution)/shard_map/ppermute | solution.py:245
  42.1 4.2 %collective-permute-done.5.refs_4_.refs_5_ = bf16[64,2048]{1,0:T(8,128)(2,1)S(1)} collective-permute-done((bf16[64,2048]{1,0:T(8,128)(2,1)S(1)}, bf16[64,2048]{1,0:T(8,128)(2,1)S(1)}, u32[]{:S(2)}, u32[]{:S(2)}) %collective-permute-start.5) | collective-permute-done | bytes 262176 | tf_op jit(solution)/shard_map/ppermute | solution.py:245
  46.3 1.7 %collective-permute-done.6.refs_5_.refs_6_ = bf16[64,2048]{1,0:T(8,128)(2,1)S(1)} collective-permute-done((bf16[64,2048]{1,0:T(8,128)(2,1)S(1)}, bf16[64,2048]{1,0:T(8,128)(2,1)S(1)}, u32[]{:S(2)}, u32[]{:S(2)}) %collective-permute-start.6) | collective-permute-done | bytes 262176 | tf_op jit(solution)/shard_map/ppermute | solution.py:245
  48.0 1.2 %all-to-all-done.1.parts = f32[8,40,128]{2,1,0:T(8,128)S(1)} async-done(((f32[8,40,128]{2,1,0:T(8,128)}), f32[8,40,128]{2,1,0:T(8,128)S(1)}, u32[]{:S(2)}, u32[]{:S(2)}) %all-to-all-start.1) | async-done | bytes 163872 | tf_op jit(solution)/shard_map/all_to_all | solution.py:251
  49.2 1.8 %vectors.5 = (bf16[2,256,128]{2,1,0:T(8,128)(2,1)S(1)}, f32[8,4096]{1,0:T(8,128)S(1)}, f32[8,4096]{1,0:T(8,128)S(1)}) custom-call(s32[3]{0:T(128)S(1)} %pad_add_fusion.place, f32[1]{0:T(128)S(6)} %copy.19.rho_ref, f32[8,40,128]{2,1,0:T(8,128)S(1)} %all-to-all-done.1.parts, f32[1,4096]{1,0:T(1,128)S(1)} %bitcast.37, s32[1,4096]{1,0:T(1,128)S(1)} %bitcast.43, ...), custom_call_target="tpu_custom_call" | custom-call | tf_op jit(solution)/shard_map/vectors/pallas_call | solution.py:263
  51.1 4.9 %collective-permute-start.8 = (bf16[2,256,128]{2,1,0:T(8,128)(2,1)S(1)}, bf16[2,256,128]{2,1,0:T(8,128)(2,1)S(1)}, u32[]{:S(2)}, u32[]{:S(2)}) collective-permute-start(bf16[2,256,128]{2,1,0:T(8,128)(2,1)S(1)} %get-tuple-element.50), channel_id=1, source_target_pairs={{0,16},{4,20},{8,24},{12,28},{16,0},{20,4},{24,8},{28,12},{1,17},{... | collective-permute-start | bytes 393224 | tf_op jit(solution)/shard_map/ppermute | solution.py:281
  56.0 2.4 %vectors.6 = (bf16[2,256,128]{2,1,0:T(8,128)(2,1)S(1)}, bf16[2,256,128]{2,1,0:T(8,128)(2,1)S(1)}) custom-call(s32[3]{0:T(128)S(1)} %pad_add_fusion.place, f32[1]{0:T(128)S(6)} %copy.19.rho_ref, f32[8,40,128]{2,1,0:T(8,128)S(1)} %all-to-all-done.1.parts, f32[1,4096]{1,0:T(1,128)S(1)} %bitcast.38, s32[1,4096]{1,0:T(1,128)S(1)} %bitcast.44, ...), custom_call_target="tpu_custom_call" | custom-call | tf_op jit(solution)/shard_map/vectors/pallas_call | solution.py:263
  59.0 2.4 %vectors.9 = (bf16[2,256,128]{2,1,0:T(8,128)(2,1)S(1)}, bf16[2,256,128]{2,1,0:T(8,128)(2,1)S(1)}) custom-call(s32[3]{0:T(128)S(1)} %pad_add_fusion.place, f32[1]{0:T(128)S(6)} %copy.19.rho_ref, f32[8,40,128]{2,1,0:T(8,128)S(1)} %all-to-all-done.1.parts, f32[1,4096]{1,0:T(1,128)S(1)} %bitcast.39, s32[1,4096]{1,0:T(1,128)S(1)} %bitcast.45, ...), custom_call_target="tpu_custom_call" | custom-call | tf_op jit(solution)/shard_map/vectors/pallas_call | solution.py:263
  61.3 2.4 %collective-permute-start.11 = (bf16[2,256,128]{2,1,0:T(8,128)(2,1)S(1)}, bf16[2,256,128]{2,1,0:T(8,128)(2,1)S(1)}, u32[]{:S(2)}, u32[]{:S(2)}) collective-permute-start(bf16[2,256,128]{2,1,0:T(8,128)(2,1)S(1)} %get-tuple-element.57), channel_id=1, source_target_pairs={{0,8},{4,12},{8,16},{12,20},{16,24},{20,28},{24,0},{28,4},{1,9},{5... | collective-permute-start | bytes 393224 | tf_op jit(solution)/shard_map/ppermute | solution.py:281
  63.8 1.8 %collective-permute-start.12 = (bf16[2,256,128]{2,1,0:T(8,128)(2,1)S(1)}, bf16[2,256,128]{2,1,0:T(8,128)(2,1)}, u32[]{:S(2)}, u32[]{:S(2)}) collective-permute-start(bf16[2,256,128]{2,1,0:T(8,128)(2,1)S(1)} %get-tuple-element.58), channel_id=1, source_target_pairs={{0,24},{4,28},{8,0},{12,4},{16,8},{20,12},{24,16},{28,20},{1,25},{... | collective-permute-start | bytes 393224 | tf_op jit(solution)/shard_map/ppermute | solution.py:281
  65.5 2.1 %collective-permute-start.13 = (bf16[2,256,128]{2,1,0:T(8,128)(2,1)S(1)}, bf16[2,256,128]{2,1,0:T(8,128)(2,1)}, u32[]{:S(2)}, u32[]{:S(2)}) collective-permute-start(bf16[2,256,128]{2,1,0:T(8,128)(2,1)S(1)} %get-tuple-element.59), channel_id=1, source_target_pairs={{0,12},{4,16},{8,20},{12,24},{16,28},{20,0},{24,4},{28,8},{1,13},{... | collective-permute-start | bytes 393224 | tf_op jit(solution)/shard_map/ppermute | solution.py:281
  67.6 2.4 %vectors.8 = (bf16[2,256,128]{2,1,0:T(8,128)(2,1)S(1)}, bf16[2,256,128]{2,1,0:T(8,128)(2,1)S(1)}) custom-call(s32[3]{0:T(128)S(1)} %pad_add_fusion.place, f32[1]{0:T(128)S(6)} %copy.19.rho_ref, f32[8,40,128]{2,1,0:T(8,128)S(1)} %all-to-all-done.1.parts, f32[1,4096]{1,0:T(1,128)S(1)} %bitcast.40, s32[1,4096]{1,0:T(1,128)S(1)} %bitcast.46, ...), custom_call_target="tpu_custom_call" | custom-call | tf_op jit(solution)/shard_map/vectors/pallas_call | solution.py:263
  70.0 1.8 %collective-permute-start.10 = (bf16[2,256,128]{2,1,0:T(8,128)(2,1)S(1)}, bf16[2,256,128]{2,1,0:T(8,128)(2,1)}, u32[]{:S(2)}, u32[]{:S(2)}) collective-permute-start(bf16[2,256,128]{2,1,0:T(8,128)(2,1)S(1)} %get-tuple-element.56), channel_id=1, source_target_pairs={{0,28},{4,0},{8,4},{12,8},{16,12},{20,16},{24,20},{28,24},{1,29},{... | collective-permute-start | bytes 393224 | tf_op jit(solution)/shard_map/ppermute | solution.py:281
  72.5 1.8 %collective-permute-start.9 = (bf16[2,256,128]{2,1,0:T(8,128)(2,1)S(1)}, bf16[2,256,128]{2,1,0:T(8,128)(2,1)}, u32[]{:S(2)}, u32[]{:S(2)}) collective-permute-start(bf16[2,256,128]{2,1,0:T(8,128)(2,1)S(1)} %get-tuple-element.55), channel_id=1, source_target_pairs={{0,4},{4,8},{8,12},{12,16},{16,20},{20,24},{24,28},{28,0},{1,5},{5... | collective-permute-start | bytes 393224 | tf_op jit(solution)/shard_map/ppermute | solution.py:281
  74.2 1.8 %vectors.7 = bf16[2,256,128]{2,1,0:T(8,128)(2,1)S(1)} custom-call(s32[3]{0:T(128)S(1)} %pad_add_fusion.place, f32[1]{0:T(128)S(6)} %copy.19.rho_ref, f32[8,40,128]{2,1,0:T(8,128)S(1)} %all-to-all-done.1.parts, f32[1,4096]{1,0:T(1,128)S(1)} %bitcast.41, s32[1,4096]{1,0:T(1,128)S(1)} %bitcast.47, f32[8,4096]{1,0:T(8,128)S(1)} %get-tuple-element.53.refs_0_, ...), custom_call_target="tpu_custom_call" | custom-call | tf_op jit(solution)/shard_map/vectors/pallas_call | solution.py:263
  76.3 3.0 %collective-permute-done.9 = bf16[2,256,128]{2,1,0:T(8,128)(2,1)} collective-permute-done((bf16[2,256,128]{2,1,0:T(8,128)(2,1)S(1)}, bf16[2,256,128]{2,1,0:T(8,128)(2,1)}, u32[]{:S(2)}, u32[]{:S(2)}) %collective-permute-start.9) | collective-permute-done | bytes 131104 | tf_op jit(solution)/shard_map/ppermute | solution.py:281
  79.6 0.9 %copy-done.5 = bf16[2,256,128]{2,1,0:T(8,128)(2,1)S(1)} copy-done((bf16[2,256,128]{2,1,0:T(8,128)(2,1)S(1)}, bf16[2,256,128]{2,1,0:T(8,128)(2,1)}, u32[]{:S(2)}) %copy-start.5) | copy-done | bytes 131096
  80.5 0.9 %bitcast_dynamic-update-slice_fusion.5 = bf16[2,8,256,128]{3,2,0,1:T(8,128)(2,1)S(1)} fusion(bf16[2,8,256,128]{3,2,0,1:T(8,128)(2,1)S(1)} %bitcast_dynamic-update-slice_fusion.6, s32[]{:T(128)S(6)} %select_n.49, bf16[2,256,128]{2,1,0:T(8,128)(2,1)} %collective-permute-done.13), kind=kLoop, calls=%fused_computation.7 | loop fusion | bytes 262148 | tf_op jit(solution)/shard_map/dynamic_update_slice | solution.py:287
  81.4 0.9 %bitcast_dynamic-update-slice_fusion.4 = bf16[2,8,256,128]{3,2,0,1:T(8,128)(2,1)S(1)} fusion(bf16[2,8,256,128]{3,2,0,1:T(8,128)(2,1)S(1)} %bitcast_dynamic-update-slice_fusion.5, s32[]{:T(128)S(6)} %select_n.50, bf16[2,256,128]{2,1,0:T(8,128)(2,1)} %collective-permute-done.12), kind=kLoop, calls=%fused_computation.6 | loop fusion | bytes 262148 | tf_op jit(solution)/shard_map/dynamic_update_slice | solution.py:287
  82.5 0.9 %bitcast_dynamic-update-slice_fusion.2 = bf16[2,8,256,128]{3,2,1,0:T(8,128)(2,1)S(1)} fusion(bf16[2,8,256,128]{3,2,1,0:T(8,128)(2,1)S(1)} %bitcast_dynamic-update-slice_fusion.3, s32[]{:T(128)S(6)} %select_n.52, bf16[2,256,128]{2,1,0:T(8,128)(2,1)} %collective-permute-done.10), kind=kLoop, calls=%fused_computation.4 | loop fusion | bytes 262148 | tf_op jit(solution)/shard_map/dynamic_update_slice | solution.py:287
  83.4 0.9 %bitcast_dynamic-update-slice_fusion.1 = bf16[2,8,256,128]{3,2,1,0:T(8,128)(2,1)S(1)} fusion(bf16[2,8,256,128]{3,2,1,0:T(8,128)(2,1)S(1)} %bitcast_dynamic-update-slice_fusion.2, s32[]{:T(128)S(6)} %select_n.53, bf16[2,256,128]{2,1,0:T(8,128)(2,1)} %collective-permute-done.9), kind=kLoop, calls=%fused_computation.3 | loop fusion | bytes 262148 | tf_op jit(solution)/shard_map/dynamic_update_slice | solution.py:287
  84.4 1.0 %copy-done.3 = bf16[2,8,256,128]{3,2,1,0:T(8,128)(2,1)} copy-done((bf16[2,8,256,128]{3,2,1,0:T(8,128)(2,1)}, bf16[2,8,256,128]{3,2,1,0:T(8,128)(2,1)S(1)}, u32[]{:S(2)}) %copy-start.3) | copy-done | bytes 1048600
  (36 shorter events, 6.1 us)
Async XLA Ops:
  0.6 16.1 %collective-permute-start = (bf16[2,64,2048]{2,1,0:T(8,128)(2,1)}, bf16[2,64,2048]{2,1,0:T(8,128)(2,1)S(1)}, u32[]{:S(2)}, u32[]{:S(2)}) collective-permute-start(bf16[2,64,2048]{2,1,0:T(8,128)(2,1)} %refs_2_.7), channel_id=1, source_target_pairs={{0,1},{1,2},{2,3},{3,0},{4,5},{5,6},{6,7},{7,4},{8,9},{9,10},{10,1... | collective-permute-start | bytes 1572872 | tf_op jit(solution)/shard_map/ppermute | solution.py:213
  2.2 14.5 %collective-permute-start.1 = (bf16[2,64,2048]{2,1,0:T(8,128)(2,1)}, bf16[2,64,2048]{2,1,0:T(8,128)(2,1)S(1)}, u32[]{:S(2)}, u32[]{:S(2)}) collective-permute-start(bf16[2,64,2048]{2,1,0:T(8,128)(2,1)} %refs_2_.7), channel_id=1, source_target_pairs={{0,3},{1,0},{2,1},{3,2},{4,7},{5,4},{6,5},{7,6},{8,11},{9,8},{10,9... | collective-permute-start | bytes 1572872 | tf_op jit(solution)/shard_map/ppermute | solution.py:214
  4.2 20.6 %copy-start.1 = (f32[4096]{0:T(1024)S(1)}, f32[4096]{0:T(1024)}, u32[]{:S(2)}) copy-start(f32[4096]{0:T(1024)} %param.6) | copy-start | bytes 49156
  4.2 20.6 %copy-start.2 = (s32[4096]{0:T(1024)S(1)}, s32[4096]{0:T(1024)}, u32[]{:S(2)}) copy-start(s32[4096]{0:T(1024)} %param.7) | copy-start | bytes 49156
  4.2 20.6 %all-to-all-start = ((bf16[32,16,128]{2,1,0:T(8,128)(2,1)}), bf16[32,16,128]{2,1,0:T(8,128)(2,1)S(1)}, u32[]{:S(2)}, u32[]{:S(2)}) async-start(bf16[32,16,128]{2,1,0:T(8,128)(2,1)} %broadcast_in_dim.35), calls=%async_computation | async-start | bytes 262144 | tf_op jit(solution)/shard_map/all_to_all | solution.py:219
  28.5 5.3 %collective-permute-start.2 = (f32[40,128]{1,0:T(8,128)S(1)}, f32[40,128]{1,0:T(8,128)S(1)}, u32[]{:S(2)}, u32[]{:S(2)}) collective-permute-start(f32[40,128]{1,0:T(8,128)S(1)} %get-tuple-element.38), channel_id=1, source_target_pairs={{0,2},{1,3},{2,0},{3,1},{4,6},{5,7},{6,4},{7,5},{8,10},{9,11},{10,... | collective-permute-start | bytes 61448 | tf_op jit(solution)/shard_map/ppermute | solution.py:243
  30.7 3.8 %collective-permute-start.3 = (f32[40,128]{1,0:T(8,128)S(1)}, f32[40,128]{1,0:T(8,128)S(1)}, u32[]{:S(2)}, u32[]{:S(2)}) collective-permute-start(f32[40,128]{1,0:T(8,128)S(1)} %get-tuple-element.38), channel_id=1, source_target_pairs={{0,1},{1,2},{2,3},{3,0},{4,5},{5,6},{6,7},{7,4},{8,9},{9,10},{10,1... | collective-permute-start | bytes 61448 | tf_op jit(solution)/shard_map/ppermute | solution.py:243
  31.9 3.8 %collective-permute-start.4 = (f32[40,128]{1,0:T(8,128)S(1)}, f32[40,128]{1,0:T(8,128)S(1)}, u32[]{:S(2)}, u32[]{:S(2)}) collective-permute-start(f32[40,128]{1,0:T(8,128)S(1)} %get-tuple-element.38), channel_id=1, source_target_pairs={{0,3},{1,0},{2,1},{3,2},{4,7},{5,4},{6,5},{7,6},{8,11},{9,8},{10,9... | collective-permute-start | bytes 61448 | tf_op jit(solution)/shard_map/ppermute | solution.py:243
  36.5 12.7 %all-to-all-start.1 = ((f32[8,40,128]{2,1,0:T(8,128)}), f32[8,40,128]{2,1,0:T(8,128)S(1)}, u32[]{:S(2)}, u32[]{:S(2)}) async-start(f32[8,40,128]{2,1,0:T(8,128)} %broadcast_in_dim.37), calls=%async_computation.1 | async-start | bytes 327680 | tf_op jit(solution)/shard_map/all_to_all | solution.py:251
  39.9 9.4 %copy-start = (bf16[2,64,2048]{2,1,0:T(8,128)(2,1)S(1)}, bf16[2,64,2048]{2,1,0:T(8,128)(2,1)}, u32[]{:S(2)}) copy-start(bf16[2,64,2048]{2,1,0:T(8,128)(2,1)} %refs_2_.7) | copy-start | bytes 1572868
  39.9 6.4 %collective-permute-start.5 = (bf16[64,2048]{1,0:T(8,128)(2,1)S(1)}, bf16[64,2048]{1,0:T(8,128)(2,1)S(1)}, u32[]{:S(2)}, u32[]{:S(2)}) collective-permute-start(bf16[64,2048]{1,0:T(8,128)(2,1)S(1)} %slice_bitcast_fusion.1), channel_id=1, source_target_pairs={{0,1},{1,2},{2,3},{3,0},{4,5},{5,6},{6,7},{7,4},{8,9},{9,10},{10,1... | collective-permute-start | bytes 786440 | tf_op jit(solution)/shard_map/ppermute | solution.py:245
  40.7 7.3 %collective-permute-start.6 = (bf16[64,2048]{1,0:T(8,128)(2,1)S(1)}, bf16[64,2048]{1,0:T(8,128)(2,1)S(1)}, u32[]{:S(2)}, u32[]{:S(2)}) collective-permute-start(bf16[64,2048]{1,0:T(8,128)(2,1)S(1)} %slice_bitcast_fusion), channel_id=1, source_target_pairs={{0,3},{1,0},{2,1},{3,2},{4,7},{5,4},{6,5},{7,6},{8,11},{9,8},{10,9... | collective-permute-start | bytes 786440 | tf_op jit(solution)/shard_map/ppermute | solution.py:245
  51.1 16.6 %collective-permute-start.8 = (bf16[2,256,128]{2,1,0:T(8,128)(2,1)S(1)}, bf16[2,256,128]{2,1,0:T(8,128)(2,1)S(1)}, u32[]{:S(2)}, u32[]{:S(2)}) collective-permute-start(bf16[2,256,128]{2,1,0:T(8,128)(2,1)S(1)} %get-tuple-element.50), channel_id=1, source_target_pairs={{0,16},{4,20},{8,24},{12,28},{16,0},{20,4},{24,8},{28,12},{1,17},{... | collective-permute-start | bytes 393224 | tf_op jit(solution)/shard_map/ppermute | solution.py:281
  58.3 13.5 %collective-permute-start.7 = (bf16[2,256,128]{2,1,0:T(8,128)(2,1)S(1)}, bf16[2,256,128]{2,1,0:T(8,128)(2,1)S(1)}, u32[]{:S(2)}, u32[]{:S(2)}) collective-permute-start(bf16[2,256,128]{2,1,0:T(8,128)(2,1)S(1)} %get-tuple-element.49), channel_id=1, source_target_pairs={{0,20},{4,24},{8,28},{12,0},{16,4},{20,8},{24,12},{28,16},{1,21},{... | collective-permute-start | bytes 393224 | tf_op jit(solution)/shard_map/ppermute | solution.py:281
  61.3 14.8 %collective-permute-start.11 = (bf16[2,256,128]{2,1,0:T(8,128)(2,1)S(1)}, bf16[2,256,128]{2,1,0:T(8,128)(2,1)S(1)}, u32[]{:S(2)}, u32[]{:S(2)}) collective-permute-start(bf16[2,256,128]{2,1,0:T(8,128)(2,1)S(1)} %get-tuple-element.57), channel_id=1, source_target_pairs={{0,8},{4,12},{8,16},{12,20},{16,24},{20,28},{24,0},{28,4},{1,9},{5... | collective-permute-start | bytes 393224 | tf_op jit(solution)/shard_map/ppermute | solution.py:281
  63.8 12.3 %collective-permute-start.12 = (bf16[2,256,128]{2,1,0:T(8,128)(2,1)S(1)}, bf16[2,256,128]{2,1,0:T(8,128)(2,1)}, u32[]{:S(2)}, u32[]{:S(2)}) collective-permute-start(bf16[2,256,128]{2,1,0:T(8,128)(2,1)S(1)} %get-tuple-element.58), channel_id=1, source_target_pairs={{0,24},{4,28},{8,0},{12,4},{16,8},{20,12},{24,16},{28,20},{1,25},{... | collective-permute-start | bytes 393224 | tf_op jit(solution)/shard_map/ppermute | solution.py:281
  65.5 10.6 %collective-permute-start.13 = (bf16[2,256,128]{2,1,0:T(8,128)(2,1)S(1)}, bf16[2,256,128]{2,1,0:T(8,128)(2,1)}, u32[]{:S(2)}, u32[]{:S(2)}) collective-permute-start(bf16[2,256,128]{2,1,0:T(8,128)(2,1)S(1)} %get-tuple-element.59), channel_id=1, source_target_pairs={{0,12},{4,16},{8,20},{12,24},{16,28},{20,0},{24,4},{28,8},{1,13},{... | collective-permute-start | bytes 393224 | tf_op jit(solution)/shard_map/ppermute | solution.py:281
  70.0 6.3 %collective-permute-start.10 = (bf16[2,256,128]{2,1,0:T(8,128)(2,1)S(1)}, bf16[2,256,128]{2,1,0:T(8,128)(2,1)}, u32[]{:S(2)}, u32[]{:S(2)}) collective-permute-start(bf16[2,256,128]{2,1,0:T(8,128)(2,1)S(1)} %get-tuple-element.56), channel_id=1, source_target_pairs={{0,28},{4,0},{8,4},{12,8},{16,12},{20,16},{24,20},{28,24},{1,29},{... | collective-permute-start | bytes 393224 | tf_op jit(solution)/shard_map/ppermute | solution.py:281
  71.8 0.7 copy-start.4
  72.5 6.8 %collective-permute-start.9 = (bf16[2,256,128]{2,1,0:T(8,128)(2,1)S(1)}, bf16[2,256,128]{2,1,0:T(8,128)(2,1)}, u32[]{:S(2)}, u32[]{:S(2)}) collective-permute-start(bf16[2,256,128]{2,1,0:T(8,128)(2,1)S(1)} %get-tuple-element.55), channel_id=1, source_target_pairs={{0,4},{4,8},{8,12},{12,16},{16,20},{20,24},{24,28},{28,0},{1,5},{5... | collective-permute-start | bytes 393224 | tf_op jit(solution)/shard_map/ppermute | solution.py:281
  79.5 0.9 %copy-start.5 = (bf16[2,256,128]{2,1,0:T(8,128)(2,1)S(1)}, bf16[2,256,128]{2,1,0:T(8,128)(2,1)}, u32[]{:S(2)}) copy-start(bf16[2,256,128]{2,1,0:T(8,128)(2,1)} %copy-done.4) | copy-start | bytes 393220
  84.4 1.0 %copy-start.3 = (bf16[2,8,256,128]{3,2,1,0:T(8,128)(2,1)}, bf16[2,8,256,128]{3,2,1,0:T(8,128)(2,1)S(1)}, u32[]{:S(2)}) copy-start(bf16[2,8,256,128]{3,2,1,0:T(8,128)(2,1)S(1)} %bitcast_dynamic-update-slice_fusion) | copy-start | bytes 3145732
